TPU v7x, 128 devices: a whole 4x4x4 slice. The times are simulated.
128 devices in a mesh: dp: 4 (over z_lo, core), dap: 32 (over x, z_hi, y).
Axes of the slice: x: 4, y: 4, z: 4 (z_hi: 2, z_lo: 2; z = z_hi * 2 + z_lo), core: 2. Of those that a mesh axis runs over, the one named last changes fastest.
Arguments:
- alignment_state: bfloat16 [1024, 512, 256], P(('dp', 'dap')), parts along dimension 0, may hold values from -6 to 6
- token_index_grid: int32 [1024, 512], P(('dp', 'dap')), parts along dimension 0, may hold values from 0 to 22
- sequence_mask: int32 [1024], P('dp'), parts along dimension 0, may hold values from 0 to 1, as said below
- residue_mask: int32 [2048], P('dp'), parts along dimension 0, may hold values from 0 to 1, as said below
- pair_state: bfloat16 [2048, 512, 128], P(('dp', 'dap')), parts along dimension 0, may hold values from -6 to 6
- token_embedding_table: bfloat16 [23, 256], replicated, may hold values from -6 to 6
- pair_bias_weight: bfloat16 [128, 8], replicated, may hold values from -0.5 to 0.5
- row_query_weight: bfloat16 [256, 256], replicated, may hold values from -10 to 10
- row_key_weight: bfloat16 [256, 256], replicated, may hold values from -10 to 10
- row_value_weight: bfloat16 [256, 256], replicated, may hold values from -0.375 to 0.375
- row_gate_weight: bfloat16 [256, 256], replicated, may hold values from -0.375 to 0.375
- row_output_weight: bfloat16 [256, 256], replicated, may hold values from -0.375 to 0.375
- column_query_weight: bfloat16 [256, 256], replicated, may hold values from -10 to 10
- column_key_weight: bfloat16 [256, 256], replicated, may hold values from -10 to 10
- column_value_weight: bfloat16 [256, 256], replicated, may hold values from -0.375 to 0.375
- column_gate_weight: bfloat16 [256, 256], replicated, may hold values from -0.375 to 0.375
- column_output_weight: bfloat16 [256, 256], replicated, may hold values from -0.375 to 0.375
Outputs:
- msa_out: bfloat16 [1024, 512, 256], P('dp', 'dap'), parts along dimension 0
There are 4 independent parts, one for each index of `dp`. A program takes and returns all parts, laid end to end along the dimension named above; an argument that names none is the same for every part. Nothing has to cross between parts.
Inputs may be any that keep to these rules, and one draw needn't show every extreme that they name: `sequence_mask`: entry 0 is 1 and the last entry is 0. `residue_mask`: entry 0 is 1 and the last entry is 0.
All inputs are finite; a program needn't handle non-finite values.
Results may differ from a plain program's by a relative error of at most 0.013.
Values may be sent and summed in bfloat16 or wider, within the bound.
A program may use at most 192 MiB of HBM per device.

v0:
```python
import jax
import jax.numpy as jnp
from jax import lax
from jax.sharding import PartitionSpec as P

HEADS = 8
HEAD_DIM = 32
TOKEN_KINDS = 23


EPSILON = 1e-05


def normalize(values):
    centered = values - jnp.mean(values, axis=-1, keepdims=True)
    variance = jnp.mean(centered * centered, axis=-1, keepdims=True)
    return centered * lax.rsqrt(variance + EPSILON)


def split_heads(projected):
    return projected.reshape(projected.shape[:-1] + (HEADS, HEAD_DIM))


def project_all(normed, w_query, w_key, w_value, w_gate):
    queries = (
        jnp.dot(normed, w_query, preferred_element_type=jnp.float32) * HEAD_DIM ** (-0.5)
    ).astype(jnp.bfloat16)
    keyed = jnp.dot(normed, w_key, preferred_element_type=jnp.float32).astype(jnp.bfloat16)
    valued = jnp.dot(normed, w_value, preferred_element_type=jnp.float32).astype(jnp.bfloat16)
    gating = jax.nn.sigmoid(jnp.dot(normed, w_gate, preferred_element_type=jnp.float32))
    return (split_heads(queries), split_heads(keyed), split_heads(valued), gating)


def attend_block(queries, keyed, valued, bias_rows, key_mask):
    scores = jnp.einsum("bqhd,bkhd->bhqk", queries, keyed, preferred_element_type=jnp.float32)
    if bias_rows is not None:
        scores = scores + bias_rows[None].astype(jnp.float32)
    scores = jnp.where(key_mask[None, None, None, :] > 0, scores, -1000000000.0)
    attn_probs = jax.nn.softmax(scores, axis=-1).astype(jnp.bfloat16)
    attended = jnp.einsum("bhqk,bkhd->bqhd", attn_probs, valued, preferred_element_type=jnp.float32)
    return attended.reshape(attended.shape[:2] + (HEADS * HEAD_DIM,))


def grouped_attend(queries, keyed, valued, bias_rows, key_mask, largest):
    count = queries.shape[0]
    group_size = 1
    for candidate in (largest, 4, 2):
        if candidate <= largest and count % candidate == 0 and (group_size == 1):
            group_size = candidate

    def regroup_lines(array):
        return array.reshape((count // group_size, group_size) + array.shape[1:])

    def one_group(item):
        group_queries, group_keyed, group_valued = item
        return attend_block(group_queries, group_keyed, group_valued, bias_rows, key_mask)

    results = lax.map(
        one_group, (regroup_lines(queries), regroup_lines(keyed), regroup_lines(valued))
    )
    return results.reshape((count,) + results.shape[2:])


def body(
    alignment_state,
    token_index_grid,
    sequence_mask,
    residue_mask,
    pair_state,
    token_embedding_table,
    pair_bias_weight,
    row_query_weight,
    row_key_weight,
    row_value_weight,
    row_gate_weight,
    row_output_weight,
    column_query_weight,
    column_key_weight,
    column_value_weight,
    column_gate_weight,
    column_output_weight,
):
    token_indicator = (
        token_index_grid[..., None] == jnp.arange(TOKEN_KINDS, dtype=jnp.int32)
    ).astype(jnp.bfloat16)
    token_embedded = alignment_state.astype(jnp.float32) + jnp.dot(
        token_indicator, token_embedding_table, preferred_element_type=jnp.float32
    )
    row_normed = normalize(token_embedded).astype(jnp.bfloat16)
    pair_normed = normalize(pair_state.astype(jnp.float32)).astype(jnp.bfloat16)
    bias_local = jnp.einsum(
        "qkc,ch->hqk", pair_normed, pair_bias_weight, preferred_element_type=jnp.float32
    ).astype(jnp.bfloat16)
    queries, keyed, valued, gating = project_all(
        row_normed, row_query_weight, row_key_weight, row_value_weight, row_gate_weight
    )
    full_bias = lax.all_gather(bias_local, "dap", axis=1, tiled=True)
    row_attended = grouped_attend(queries, keyed, valued, full_bias, residue_mask, 2)
    row_mixed = (row_attended * gating).astype(jnp.bfloat16)
    updated = (
        token_embedded + jnp.dot(row_mixed, row_output_weight, preferred_element_type=jnp.float32)
    ).astype(jnp.bfloat16)
    seq_count, res_count, channels = updated.shape
    peers = lax.axis_size("dap")
    blocks = updated.reshape(seq_count, peers, res_count // peers, channels)
    regrouped = lax.all_to_all(blocks, "dap", split_axis=1, concat_axis=0, tiled=True)
    whole_cols = regrouped.reshape(regrouped.shape[0], regrouped.shape[2], channels)
    by_residue = jnp.moveaxis(whole_cols, 1, 0)
    normed = normalize(by_residue.astype(jnp.float32)).astype(jnp.bfloat16)
    col_queries, col_keyed, col_valued, col_gating = project_all(
        normed, column_query_weight, column_key_weight, column_value_weight, column_gate_weight
    )
    attended = grouped_attend(col_queries, col_keyed, col_valued, None, sequence_mask, 4)
    col_mixed = (attended * col_gating).astype(jnp.bfloat16)
    result = jnp.dot(col_mixed, column_output_weight, preferred_element_type=jnp.float32)
    finished = (by_residue.astype(jnp.float32) + result).astype(jnp.bfloat16)
    return jnp.moveaxis(finished, 0, 1)


def solution(mesh):
    in_specs = (
        P(("dp", "dap"), None, None),
        P(("dp", "dap"), None),
        P("dp"),
        P("dp"),
        P(("dp", "dap"), None, None),
        P(),
        P(),
        P(),
        P(),
        P(),
        P(),
        P(),
        P(),
        P(),
        P(),
        P(),
        P(),
    )
    out_specs = P("dp", "dap", None)
    return jax.shard_map(body, mesh=mesh, in_specs=in_specs, out_specs=out_specs, check_vma=False)
```

profile of v0, /device:TPU:0, one launch (start us, length us, event | category | flops | bytes accessed | tf_op | source)
XLA Modules:
  0.0 355.1 jit_solution(7665201453241222503)
XLA Ops:
  6.6 2.4 convert_reduce_fusion
  9.0 3.6 %fusion.73 = f32[16,512]{1,0:T(8,128)S(1)} fusion(bf16[16,512,128]{2,1,0:T(8,128)(2,1)} %param.25, f32[16,512]{1,0:T(8,128)S(1)} %broadcast_multiply_fusion), kind=kLoop, calls=%fused_computation.57 | loop fusion | flops 4186112 | bytes 2162688 | tf_op jit(solution)/shard_map/reduce_sum | solution.py:16
  12.6 3.5 fusion.83
  16.2 2.9 fusion.121
  19.1 1.3 multiply_reduce_fusion.1
  20.5 1.8 convolution_convert_fusion.2
  22.3 2.9 multiply_convert_fusion.4
  25.3 2.9 convolution_convert_fusion.3
  28.2 73.2 %all-gather.2.cloned.1.call-done = bf16[8,512,512]{2,0,1:T(8,128)(2,1)} async-done(((bf16[8,16,512]{2,0,1:T(8,128)(2,1)}), bf16[8,512,512]{2,0,1:T(8,128)(2,1)}) %all-gather.2.cloned.1.call-update) | async-done | bytes 4194320 | tf_op jit(solution)/shard_map/all_gather | solution.py:97
  101.4 7.6 %copy.36 = bf16[8,512,512]{1,2,0:T(8,128)(2,1)} copy(bf16[8,512,512]{2,0,1:T(8,128)(2,1)} %all-gather.2.cloned.1.call-done) | data formatting | bytes 8388608 | tf_op jit(solution)/shard_map/while | solution.py:58
  108.9 107.0 %while.20 = (s32[]{:T(128)}, f32[4,2,512,256]{2,3,1,0:T(8,128)}, bf16[4,2,512,8,32]{2,4,3,1,0:T(8,128)(2,1)}, s32[512]{0:T(512)S(1)}, bf16[4,2,512,8,32]{2,4,3,1...) while((s32[]{:T(128)}, f32[4,2,512,256]{2,3,1,0:T(8,128)}, ...), condition=%wide.region_7.8_spmd, body=%wide.region_4.7_spmd.sunk | while | flops 564134912 | bytes 59315284 | solution.py:58
  108.9 6.6 %convert_element_type.178 = f32[8,512,512]{1,2,0:T(8,128)} convert(bf16[8,512,512]{1,2,0:T(8,128)(2,1)} %get-tuple-element.232) | non-fusion elementwise | flops 2097152 | bytes 12582912 | tf_op jit(solution)/shard_map/while/body/eval_jaxpr/convert_element_type | solution.py:37
  115.5 12.3 %fusion.135 = (f32[2,8,512]{2,1,0:T(8,128)S(1)}, f32[2,8,512,512]{2,3,1,0:T(8,128)}) fusion(f32[8,512,512]{1,2,0:T(8,128)} %convert_element_type.178, pred[512]{0:T(512)(128)(4,1)S(1)} %broadcast_compare_fusion.4, bf16[4,2,512,8,32]{2,4,3,1,0:T(8,128)(2,1)S(1)} %get-tuple-element.231, s32[]{:T(128)} %get-tuple-element.218, ...), kind=kOutput, calls=%fused_computation.105.clone.1 | convolution fusion | flops 285213184 | bytes 26248704 | tf_op jit(solution)/shard_map/while/body/eval_jaxpr/sub | solution.py:39
  127.8 6.8 %fusion.136 = f32[2,8,32,512]{3,2,1,0:T(8,128)S(1)} fusion(f32[2,8,512,512]{2,3,1,0:T(8,128)} %get-tuple-element.200, f32[2,8,512]{2,1,0:T(8,128)S(1)} %get-tuple-element.201, bf16[4,2,512,8,32]{2,4,3,1,0:T(8,128)(2,1)} %get-tuple-element.228, s32[]{:T(128)} %get-tuple-element.218), kind=kOutput, calls=%fused_computation.8.clone.1 | convolution fusion | flops 276824064 | bytes 18383360 | tf_op jit(solution)/shard_map/while/body/eval_jaxpr/bhqk,bkhd->bqhd/dot_general | solution.py:40
  135.7 6.6 %convert_element_type.178 = f32[8,512,512]{1,2,0:T(8,128)} convert(bf16[8,512,512]{1,2,0:T(8,128)(2,1)} %get-tuple-element.232) | non-fusion elementwise | flops 2097152 | bytes 12582912 | tf_op jit(solution)/shard_map/while/body/eval_jaxpr/convert_element_type | solution.py:37
  142.2 12.3 %fusion.135 = (f32[2,8,512]{2,1,0:T(8,128)S(1)}, f32[2,8,512,512]{2,3,1,0:T(8,128)}) fusion(f32[8,512,512]{1,2,0:T(8,128)} %convert_element_type.178, pred[512]{0:T(512)(128)(4,1)S(1)} %broadcast_compare_fusion.4, bf16[4,2,512,8,32]{2,4,3,1,0:T(8,128)(2,1)S(1)} %get-tuple-element.231, s32[]{:T(128)} %get-tuple-element.218, ...), kind=kOutput, calls=%fused_computation.105.clone.1 | convolution fusion | flops 285213184 | bytes 26248704 | tf_op jit(solution)/shard_map/while/body/eval_jaxpr/sub | solution.py:39
  154.5 6.8 %fusion.136 = f32[2,8,32,512]{3,2,1,0:T(8,128)S(1)} fusion(f32[2,8,512,512]{2,3,1,0:T(8,128)} %get-tuple-element.200, f32[2,8,512]{2,1,0:T(8,128)S(1)} %get-tuple-element.201, bf16[4,2,512,8,32]{2,4,3,1,0:T(8,128)(2,1)} %get-tuple-element.228, s32[]{:T(128)} %get-tuple-element.218), kind=kOutput, calls=%fused_computation.8.clone.1 | convolution fusion | flops 276824064 | bytes 18383360 | tf_op jit(solution)/shard_map/while/body/eval_jaxpr/bhqk,bkhd->bqhd/dot_general | solution.py:40
  161.3 1.1 constant_dynamic-update-slice_fusion.4
  162.4 6.6 %convert_element_type.178 = f32[8,512,512]{1,2,0:T(8,128)} convert(bf16[8,512,512]{1,2,0:T(8,128)(2,1)} %get-tuple-element.232) | non-fusion elementwise | flops 2097152 | bytes 12582912 | tf_op jit(solution)/shard_map/while/body/eval_jaxpr/convert_element_type | solution.py:37
  169.0 12.3 %fusion.135 = (f32[2,8,512]{2,1,0:T(8,128)S(1)}, f32[2,8,512,512]{2,3,1,0:T(8,128)}) fusion(f32[8,512,512]{1,2,0:T(8,128)} %convert_element_type.178, pred[512]{0:T(512)(128)(4,1)S(1)} %broadcast_compare_fusion.4, bf16[4,2,512,8,32]{2,4,3,1,0:T(8,128)(2,1)S(1)} %get-tuple-element.231, s32[]{:T(128)} %get-tuple-element.218, ...), kind=kOutput, calls=%fused_computation.105.clone.1 | convolution fusion | flops 285213184 | bytes 26248704 | tf_op jit(solution)/shard_map/while/body/eval_jaxpr/sub | solution.py:39
  181.3 6.8 %fusion.136 = f32[2,8,32,512]{3,2,1,0:T(8,128)S(1)} fusion(f32[2,8,512,512]{2,3,1,0:T(8,128)} %get-tuple-element.200, f32[2,8,512]{2,1,0:T(8,128)S(1)} %get-tuple-element.201, bf16[4,2,512,8,32]{2,4,3,1,0:T(8,128)(2,1)} %get-tuple-element.228, s32[]{:T(128)} %get-tuple-element.218), kind=kOutput, calls=%fused_computation.8.clone.1 | convolution fusion | flops 276824064 | bytes 18383360 | tf_op jit(solution)/shard_map/while/body/eval_jaxpr/bhqk,bkhd->bqhd/dot_general | solution.py:40
  189.2 6.6 %convert_element_type.178 = f32[8,512,512]{1,2,0:T(8,128)} convert(bf16[8,512,512]{1,2,0:T(8,128)(2,1)} %get-tuple-element.232) | non-fusion elementwise | flops 2097152 | bytes 12582912 | tf_op jit(solution)/shard_map/while/body/eval_jaxpr/convert_element_type | solution.py:37
  195.7 12.3 %fusion.135 = (f32[2,8,512]{2,1,0:T(8,128)S(1)}, f32[2,8,512,512]{2,3,1,0:T(8,128)}) fusion(f32[8,512,512]{1,2,0:T(8,128)} %convert_element_type.178, pred[512]{0:T(512)(128)(4,1)S(1)} %broadcast_compare_fusion.4, bf16[4,2,512,8,32]{2,4,3,1,0:T(8,128)(2,1)S(1)} %get-tuple-element.231, s32[]{:T(128)} %get-tuple-element.218, ...), kind=kOutput, calls=%fused_computation.105.clone.1 | convolution fusion | flops 285213184 | bytes 26248704 | tf_op jit(solution)/shard_map/while/body/eval_jaxpr/sub | solution.py:39
  208.1 6.8 %fusion.136 = f32[2,8,32,512]{3,2,1,0:T(8,128)S(1)} fusion(f32[2,8,512,512]{2,3,1,0:T(8,128)} %get-tuple-element.200, f32[2,8,512]{2,1,0:T(8,128)S(1)} %get-tuple-element.201, bf16[4,2,512,8,32]{2,4,3,1,0:T(8,128)(2,1)} %get-tuple-element.228, s32[]{:T(128)} %get-tuple-element.218), kind=kOutput, calls=%fused_computation.8.clone.1 | convolution fusion | flops 276824064 | bytes 18383360 | tf_op jit(solution)/shard_map/while/body/eval_jaxpr/bhqk,bkhd->bqhd/dot_general | solution.py:40
  214.8 1.1 constant_dynamic-update-slice_fusion.4
  216.0 5.4 %copy.37 = f32[8,512,256]{2,1,0:T(8,128)} copy(f32[8,512,256]{1,2,0:T(8,128)} %bitcast.19) | data formatting | bytes 8388608 | tf_op jit(solution)/shard_map/reshape | solution.py:61
  221.4 5.9 %add_convert_fusion = bf16[8,512,256]{2,1,0:T(8,128)(2,1)S(1)} fusion(f32[8,512,256]{2,1,0:T(8,128)} %copy-done.3, f32[8,512,256]{2,1,0:T(8,128)} %copy.37, bf16[256,256]{1,0:T(8,128)(2,1)S(1)} %copy-done.17, bf16[256,256]{1,0:T(8,128)(2,1)S(1)} %copy-done.18, f32[8,512]{1,0:T(8,128)S(1)} %copy-done.8, f32[8,512]{1,0:T(8,128)S(1)} %copy-done.6), kind=kOutput, calls=%fused_computation.68 | convolution fusion | flops 1084227584 | bytes 10780672 | tf_op jit(solution)/shard_map/dot_general | solution.py:101
  227.3 1.6 copy.38
  228.9 4.6 %all-to-all-start = ((bf16[8,32,16,256]{3,2,0,1:T(8,128)(2,1)}), bf16[8,32,16,256]{3,2,0,1:T(8,128)(2,1)S(1)}, u32[]{:S(2)}, u32[]{:S(2)}) async-start(bf16[8,32,16,256]{3,2,0,1:T(8,128)(2,1)} %copy.38), calls=%async_computation | async-start | bytes 4194304 | tf_op jit(solution)/shard_map/all_to_all | solution.py:106
  233.5 27.0 %all-to-all-done = bf16[8,32,16,256]{3,2,0,1:T(8,128)(2,1)S(1)} async-done(((bf16[8,32,16,256]{3,2,0,1:T(8,128)(2,1)}), bf16[8,32,16,256]{3,2,0,1:T(8,128)(2,1)S(1)}, u32[]{:S(2)}, u32[]{:S(2)}) %all-to-all-start) | async-done | bytes 2097184 | tf_op jit(solution)/shard_map/all_to_all | solution.py:106
  261.1 2.3 bitcast_reduce_fusion
  263.5 3.2 multiply_reduce_fusion
  266.8 3.0 convolution_convert_fusion
  269.8 4.1 %multiply_convert_fusion.1 = bf16[16,256,256]{1,2,0:T(8,128)(2,1)} fusion(bf16[256,256]{1,0:T(8,128)(2,1)S(1)} %copy-done.12, f32[32,8,1,16,256]{4,3,1,0,2:T(8,128)S(1)} %convert_bitcast_fusion, f32[16,256]{1,0:T(8,128)S(1)} %add_rsqrt_fusion.1, f32[16,256]{1,0:T(8,128)S(1)} %broadcast_multiply_fusion.1), kind=kOutput, calls=%fused_computation.65 | convolution fusion | flops 542113792 | bytes 6455296 | tf_op jit(solution)/shard_map/dot_general | solution.py:26
  273.9 4.0 %convolution_convert_fusion.1 = bf16[16,256,256]{1,2,0:T(8,128)(2,1)} fusion(bf16[256,256]{1,0:T(8,128)(2,1)S(1)} %copy-done.13, f32[32,8,1,16,256]{4,3,1,0,2:T(8,128)S(1)} %convert_bitcast_fusion, f32[16,256]{1,0:T(8,128)S(1)} %add_rsqrt_fusion.1, f32[16,256]{1,0:T(8,128)S(1)} %broadcast_multiply_fusion.1), kind=kOutput, calls=%fused_computation.78 | convolution fusion | flops 541065216 | bytes 6455296 | tf_op jit(solution)/shard_map/dot_general | solution.py:29
  277.8 51.2 %while.21 = (s32[]{:T(128)}, f32[4,4,256,256]{2,3,1,0:T(8,128)}, bf16[4,4,256,8,32]{2,4,3,1,0:T(8,128)(2,1)}, s32[256]{0:T(256)S(1)}, bf16[4,4,256,8,32]{2,4,3,1...) while((s32[]{:T(128)}, f32[4,4,256,256]{2,3,1,0:T(8,128)}, ...), condition=%wide.region_13.14_spmd, body=%wide.region_10.13_spmd.sunk | while | flops 278921728 | bytes 21565260 | solution.py:58
  277.9 7.3 %fusion.140 = (f32[4,8,256]{2,1,0:T(8,128)S(1)}, f32[4,8,256,256]{2,3,1,0:T(8,128)}) fusion(pred[256]{0:T(512)(128)(4,1)S(1)} %broadcast_compare_fusion.5, bf16[4,4,256,8,32]{2,4,3,1,0:T(8,128)(2,1)S(1)} %get-tuple-element.253, s32[]{:T(128)} %get-tuple-element.241, bf16[4,4,256,8,32]{2,4,3,1,0:T(8,128)(2,1)} %get-tuple-element.252), kind=kOutput, calls=%fused_computation.106.clone.1 | convolution fusion | flops 140509440 | bytes 9471488 | tf_op jit(solution)/shard_map/while/body/eval_jaxpr/sub | solution.py:39
  285.2 4.4 %fusion.141 = f32[4,8,32,256]{3,2,1,0:T(8,128)S(1)} fusion(f32[4,8,256,256]{2,3,1,0:T(8,128)} %get-tuple-element.208, f32[4,8,256]{2,1,0:T(8,128)S(1)} %get-tuple-element.209, bf16[4,4,256,8,32]{2,4,3,1,0:T(8,128)(2,1)} %get-tuple-element.250, s32[]{:T(128)} %get-tuple-element.241), kind=kOutput, calls=%fused_computation.34.clone.1 | convolution fusion | flops 138412032 | bytes 9994752 | tf_op jit(solution)/shard_map/while/body/eval_jaxpr/bhqk,bkhd->bqhd/dot_general | solution.py:40
  289.6 1.1 constant_dynamic-update-slice_fusion.5
  290.7 7.3 %fusion.140 = (f32[4,8,256]{2,1,0:T(8,128)S(1)}, f32[4,8,256,256]{2,3,1,0:T(8,128)}) fusion(pred[256]{0:T(512)(128)(4,1)S(1)} %broadcast_compare_fusion.5, bf16[4,4,256,8,32]{2,4,3,1,0:T(8,128)(2,1)S(1)} %get-tuple-element.253, s32[]{:T(128)} %get-tuple-element.241, bf16[4,4,256,8,32]{2,4,3,1,0:T(8,128)(2,1)} %get-tuple-element.252), kind=kOutput, calls=%fused_computation.106.clone.1 | convolution fusion | flops 140509440 | bytes 9471488 | tf_op jit(solution)/shard_map/while/body/eval_jaxpr/sub | solution.py:39
  298.0 4.4 %fusion.141 = f32[4,8,32,256]{3,2,1,0:T(8,128)S(1)} fusion(f32[4,8,256,256]{2,3,1,0:T(8,128)} %get-tuple-element.208, f32[4,8,256]{2,1,0:T(8,128)S(1)} %get-tuple-element.209, bf16[4,4,256,8,32]{2,4,3,1,0:T(8,128)(2,1)} %get-tuple-element.250, s32[]{:T(128)} %get-tuple-element.241), kind=kOutput, calls=%fused_computation.34.clone.1 | convolution fusion | flops 138412032 | bytes 9994752 | tf_op jit(solution)/shard_map/while/body/eval_jaxpr/bhqk,bkhd->bqhd/dot_general | solution.py:40
  303.5 7.3 %fusion.140 = (f32[4,8,256]{2,1,0:T(8,128)S(1)}, f32[4,8,256,256]{2,3,1,0:T(8,128)}) fusion(pred[256]{0:T(512)(128)(4,1)S(1)} %broadcast_compare_fusion.5, bf16[4,4,256,8,32]{2,4,3,1,0:T(8,128)(2,1)S(1)} %get-tuple-element.253, s32[]{:T(128)} %get-tuple-element.241, bf16[4,4,256,8,32]{2,4,3,1,0:T(8,128)(2,1)} %get-tuple-element.252), kind=kOutput, calls=%fused_computation.106.clone.1 | convolution fusion | flops 140509440 | bytes 9471488 | tf_op jit(solution)/shard_map/while/body/eval_jaxpr/sub | solution.py:39
  310.8 4.4 %fusion.141 = f32[4,8,32,256]{3,2,1,0:T(8,128)S(1)} fusion(f32[4,8,256,256]{2,3,1,0:T(8,128)} %get-tuple-element.208, f32[4,8,256]{2,1,0:T(8,128)S(1)} %get-tuple-element.209, bf16[4,4,256,8,32]{2,4,3,1,0:T(8,128)(2,1)} %get-tuple-element.250, s32[]{:T(128)} %get-tuple-element.241), kind=kOutput, calls=%fused_computation.34.clone.1 | convolution fusion | flops 138412032 | bytes 9994752 | tf_op jit(solution)/shard_map/while/body/eval_jaxpr/bhqk,bkhd->bqhd/dot_general | solution.py:40
  316.3 7.3 %fusion.140 = (f32[4,8,256]{2,1,0:T(8,128)S(1)}, f32[4,8,256,256]{2,3,1,0:T(8,128)}) fusion(pred[256]{0:T(512)(128)(4,1)S(1)} %broadcast_compare_fusion.5, bf16[4,4,256,8,32]{2,4,3,1,0:T(8,128)(2,1)S(1)} %get-tuple-element.253, s32[]{:T(128)} %get-tuple-element.241, bf16[4,4,256,8,32]{2,4,3,1,0:T(8,128)(2,1)} %get-tuple-element.252), kind=kOutput, calls=%fused_computation.106.clone.1 | convolution fusion | flops 140509440 | bytes 9471488 | tf_op jit(solution)/shard_map/while/body/eval_jaxpr/sub | solution.py:39
  323.6 4.4 %fusion.141 = f32[4,8,32,256]{3,2,1,0:T(8,128)S(1)} fusion(f32[4,8,256,256]{2,3,1,0:T(8,128)} %get-tuple-element.208, f32[4,8,256]{2,1,0:T(8,128)S(1)} %get-tuple-element.209, bf16[4,4,256,8,32]{2,4,3,1,0:T(8,128)(2,1)} %get-tuple-element.250, s32[]{:T(128)} %get-tuple-element.241), kind=kOutput, calls=%fused_computation.34.clone.1 | convolution fusion | flops 138412032 | bytes 9994752 | tf_op jit(solution)/shard_map/while/body/eval_jaxpr/bhqk,bkhd->bqhd/dot_general | solution.py:40
  329.1 5.4 %copy.43 = f32[16,256,256]{2,1,0:T(8,128)} copy(f32[16,256,256]{1,2,0:T(8,128)} %bitcast.34) | data formatting | bytes 8388608 | tf_op jit(solution)/shard_map/reshape | solution.py:61
  334.5 11.2 %fusion.75 = bf16[256,16,256]{2,0,1:T(8,128)(2,1)S(1)} fusion(f32[32,8,1,16,256]{4,3,1,0,2:T(8,128)} %copy-done.2, f32[16,256,256]{2,1,0:T(8,128)} %copy.43, bf16[256,256]{1,0:T(8,128)(2,1)S(1)} %copy-done.19, bf16[256,256]{1,0:T(8,128)(2,1)S(1)} %copy-done.20, f32[16,256]{1,0:T(8,128)S(1)} %add_rsqrt_fusion.1, f32[16,256]{1,0:T(8,128)S(1)} %broadcast_multiply_fusion.1), kind=kOutput, calls=%fused_computation.61 | convolution fusion | flops 1084227584 | bytes 10780672 | tf_op jit(solution)/shard_map/dot_general | solution.py:115
  345.7 2.5 copy.44
  (70 shorter events, 6.1 us)
Async XLA Ops:
  6.5 14.0 %copy-start = (bf16[256,256]{1,0:T(8,128)(2,1)S(1)}, bf16[256,256]{1,0:T(8,128)(2,1)}, u32[]{:S(2)}) copy-start(bf16[256,256]{1,0:T(8,128)(2,1)} %param.29) | copy-start | bytes 393220
  6.5 6.1 %copy-start.4 = (bf16[16,512,128]{2,1,0:T(8,128)(2,1)S(1)}, bf16[16,512,128]{2,1,0:T(8,128)(2,1)}, u32[]{:S(2)}) copy-start(bf16[16,512,128]{2,1,0:T(8,128)(2,1)} %param.25) | copy-start | bytes 6291460
  6.5 6.1 %copy-start.21 = (bf16[128,8]{0,1:T(8,128)(2,1)S(1)}, bf16[128,8]{0,1:T(8,128)(2,1)}, u32[]{:S(2)}) copy-start(bf16[128,8]{0,1:T(8,128)(2,1)} %param.27) | copy-start | bytes 6148
  6.5 9.6 %copy-start.15 = (s32[8,512]{1,0:T(8,128)S(1)}, s32[8,512]{1,0:T(8,128)}, u32[]{:S(2)}) copy-start(s32[8,512]{1,0:T(8,128)} %param.22) | copy-start | bytes 49156
  6.5 9.7 %copy-start.16 = (bf16[23,256]{1,0:T(8,128)(2,1)S(1)}, bf16[23,256]{1,0:T(8,128)(2,1)}, u32[]{:S(2)}) copy-start(bf16[23,256]{1,0:T(8,128)(2,1)} %param.26) | copy-start | bytes 35332
  6.5 94.8 %all-gather.2.cloned.1.call-start = ((), (), s32[]{:S(2)}) async-start(), calls=%async_computation.1 | async-start | bytes 4325376 | tf_op jit(solution)/shard_map/all_gather | solution.py:97
  19.1 6.2 %copy-start.3 = (f32[8,512,256]{2,1,0:T(8,128)}, f32[8,512,256]{2,1,0:T(8,128)S(1)}, u32[]{:S(2)}) copy-start(f32[8,512,256]{2,1,0:T(8,128)S(1)} %get-tuple-element.121) | copy-start | bytes 12582916
  19.1 6.1 %copy-start.5 = (f32[8,512]{1,0:T(8,128)}, f32[8,512]{1,0:T(8,128)S(1)}, u32[]{:S(2)}) copy-start(f32[8,512]{1,0:T(8,128)S(1)} %broadcast_multiply_fusion.2) | copy-start | bytes 49156
  20.5 1.8 copy-start.9
  20.5 4.8 %copy-start.7 = (f32[8,512]{1,0:T(8,128)}, f32[8,512]{1,0:T(8,128)S(1)}, u32[]{:S(2)}) copy-start(f32[8,512]{1,0:T(8,128)S(1)} %add_rsqrt_fusion.2) | copy-start | bytes 49156
  22.3 3.0 copy-start.10
  28.2 80.7 %copy-start.14 = (s32[512]{0:T(512)S(1)}, s32[512]{0:T(512)}, u32[]{:S(2)}) copy-start(s32[512]{0:T(512)} %param.24) | copy-start | bytes 6148
  215.9 5.4 %copy-start.6 = (f32[8,512]{1,0:T(8,128)S(1)}, f32[8,512]{1,0:T(8,128)}, u32[]{:S(2)}) copy-start(f32[8,512]{1,0:T(8,128)} %copy-done.5) | copy-start | bytes 49156
  215.9 5.4 %copy-start.8 = (f32[8,512]{1,0:T(8,128)S(1)}, f32[8,512]{1,0:T(8,128)}, u32[]{:S(2)}) copy-start(f32[8,512]{1,0:T(8,128)} %copy-done.7) | copy-start | bytes 49156
  215.9 5.4 %copy-start.17 = (bf16[256,256]{1,0:T(8,128)(2,1)S(1)}, bf16[256,256]{1,0:T(8,128)(2,1)}, u32[]{:S(2)}) copy-start(bf16[256,256]{1,0:T(8,128)(2,1)} %param.32) | copy-start | bytes 393220
  215.9 5.4 %copy-start.18 = (bf16[256,256]{1,0:T(8,128)(2,1)S(1)}, bf16[256,256]{1,0:T(8,128)(2,1)}, u32[]{:S(2)}) copy-start(bf16[256,256]{1,0:T(8,128)(2,1)} %param.31) | copy-start | bytes 393220
  228.9 31.7 %all-to-all-start = ((bf16[8,32,16,256]{3,2,0,1:T(8,128)(2,1)}), bf16[8,32,16,256]{3,2,0,1:T(8,128)(2,1)S(1)}, u32[]{:S(2)}, u32[]{:S(2)}) async-start(bf16[8,32,16,256]{3,2,0,1:T(8,128)(2,1)} %copy.38), calls=%async_computation | async-start | bytes 4194304 | tf_op jit(solution)/shard_map/all_to_all | solution.py:106
  261.1 12.8 %copy-start.2 = (f32[32,8,1,16,256]{4,3,1,0,2:T(8,128)}, f32[32,8,1,16,256]{4,3,1,0,2:T(8,128)S(1)}, u32[]{:S(2)}) copy-start(f32[32,8,1,16,256]{4,3,1,0,2:T(8,128)S(1)} %convert_bitcast_fusion) | copy-start | bytes 12582916
  261.1 5.6 %copy-start.11 = (bf16[256,256]{1,0:T(8,128)(2,1)S(1)}, bf16[256,256]{1,0:T(8,128)(2,1)}, u32[]{:S(2)}) copy-start(bf16[256,256]{1,0:T(8,128)(2,1)} %param.34) | copy-start | bytes 393220
  266.7 3.1 copy-start.12
  269.8 4.1 %copy-start.13 = (bf16[256,256]{1,0:T(8,128)(2,1)S(1)}, bf16[256,256]{1,0:T(8,128)(2,1)}, u32[]{:S(2)}) copy-start(bf16[256,256]{1,0:T(8,128)(2,1)} %param.35) | copy-start | bytes 393220
  273.9 4.0 %copy-start.22 = (s32[256]{0:T(256)S(1)}, s32[256]{0:T(256)}, u32[]{:S(2)}) copy-start(s32[256]{0:T(256)} %param.23) | copy-start | bytes 3076
  329.1 5.4 %copy-start.19 = (bf16[256,256]{1,0:T(8,128)(2,1)S(1)}, bf16[256,256]{1,0:T(8,128)(2,1)}, u32[]{:S(2)}) copy-start(bf16[256,256]{1,0:T(8,128)(2,1)} %param.37) | copy-start | bytes 393220
  329.1 5.4 %copy-start.20 = (bf16[256,256]{1,0:T(8,128)(2,1)S(1)}, bf16[256,256]{1,0:T(8,128)(2,1)}, u32[]{:S(2)}) copy-start(bf16[256,256]{1,0:T(8,128)(2,1)} %param.36) | copy-start | bytes 393220
  334.5 13.7 %copy-start.1 = (bf16[256,256]{1,0:T(8,128)(2,1)S(1)}, bf16[256,256]{1,0:T(8,128)(2,1)}, u32[]{:S(2)}) copy-start(bf16[256,256]{1,0:T(8,128)(2,1)} %param.29) | copy-start | bytes 393220
Sparse Core Ops, SparseCore 0:
  16.3 85.0 all-gather.1
where the time goes:
time: 357 us; the launch traced here: 355 us
  matrix products  165 us (46%)
  waiting for transfers between devices  100 us (28%)
  other arithmetic  39.8 us (11%)
  local copies, waits for them, and re-layouts  31.2 us (9%)
  between operations  13.7 us (4%)
  starting transfers between devices  4.66 us (1%)
    sub x8, matrix products, attend_block(): attn_probs = jax.nn.softmax(scores, axis=-1).astype(jnp.bfloat16)  78.5 us
    all_gather x1, waiting for transfers between devices, body(): full_bias = lax.all_gather(bias_local, 'dap', axis=1, tiled=True)  73.2 us
    dot_general x8, matrix products, attend_block(): jnp.einsum('bhqk,bkhd->bqhd', attn_probs, valued, preferred_element_type=...  44.8 us
    all_to_all x1, waiting for transfers between devices, body(): lax.all_to_all(blocks, 'dap', split_axis=1, concat_axis=0, tiled=True)  27 us
    convert_element_type x4, other arithmetic, attend_block(): scores = scores + bias_rows[None].astype(jnp.float32)  26.3 us
    dot_general x1, matrix products, body(): jnp.dot(col_mixed, column_output_weight, preferred_element_type=jnp.float32)  11.2 us
    reshape x2, local copies, waits for them, and re-layouts, grouped_attend(): return results.reshape((count,) + results.shape[2:])  10.8 us
    dynamic_update_slice x8, local copies, waits for them, and re-layouts, grouped_attend(): lax.map(one_group, (regroup_lines(queries), regroup_lines(keyed), regroup...  8.59 us
  transfers between devices with their start and end apart: 2, of which 2 were waited for; matrix products, arithmetic and copies ran while one was open for 3% of the time, Pallas kernels for 0%

commit v1 on v0

v1 whole, which is shorter than its diff:
```python
import functools

import jax
import jax.numpy as jnp
from jax import lax
from jax.experimental import pallas as pl
from jax.experimental.pallas import tpu as pltpu
from jax.sharding import PartitionSpec as P

HEADS = 8
HEAD_DIM = 32
GROUP = 4
TOKEN_KINDS = 23
EPSILON = 1e-05
LOG2E = 1.4426950408889634
MASKED = -1e9
QUERY_ROWS = 128
VMEM_LIMIT = 60 * 1024 * 1024

NT = (((1,), (1,)), ((), ()))
TN = (((0,), (0,)), ((), ()))


def dot(a, b, dims=(((1,), (0,)), ((), ()))):
    return lax.dot_general(a, b, dims, preferred_element_type=jnp.float32)


def normalize(values):
    centered = values - jnp.mean(values, axis=-1, keepdims=True)
    variance = jnp.mean(centered * centered, axis=-1, keepdims=True)
    return centered * lax.rsqrt(variance + EPSILON)


def sigmoid(x):
    return 0.5 * jnp.tanh(0.5 * x) + 0.5


def lane_head(shape):
    return lax.broadcasted_iota(jnp.int32, shape, len(shape) - 1) // HEAD_DIM


def bias_kernel(pair_ref, weight_ref, out_ref):
    rows = pair_ref.shape[0]
    channels = pair_ref.shape[2]
    weight = weight_ref[...]
    averaging = jnp.full((channels, channels), 1.0 / channels, jnp.bfloat16)
    for row in range(rows):
        block = pair_ref[row]
        centered = block.astype(jnp.float32) - dot(block, averaging)
        variance = dot((centered * centered).astype(jnp.bfloat16), averaging)
        normed = (centered * lax.rsqrt(variance + EPSILON)).astype(jnp.bfloat16)
        projected = dot(weight, normed, (((0,), (1,)), ((), ())))
        out_ref[:, row, :] = projected.astype(jnp.bfloat16)


def pair_bias(pair_state, weight):
    rows, keys, channels = pair_state.shape
    return pl.pallas_call(
        bias_kernel,
        out_shape=jax.ShapeDtypeStruct((HEADS, rows, keys), jnp.bfloat16),
        in_specs=[pl.BlockSpec(memory_space=pltpu.VMEM)] * 2,
        out_specs=pl.BlockSpec(memory_space=pltpu.VMEM),
        compiler_params=pltpu.CompilerParams(vmem_limit_bytes=VMEM_LIMIT),
        name="pair_bias",
    )(pair_state, weight)


def store_keys(key_ref, index, keyed):
    lanes = lane_head((1, 128))
    for head in range(HEADS):
        part = keyed[:, 128 * (head // GROUP):128 * (head // GROUP + 1)]
        key_ref[index, head] = jnp.where(lanes == head % GROUP, part, 0.0).astype(jnp.bfloat16)


def store_values(value_ref, index, valued, live):
    lanes = lane_head((1, 128))
    for head in range(HEADS):
        part = valued[:, 128 * (head // GROUP):128 * (head // GROUP + 1)]
        mine = lanes == head % GROUP
        value_ref[index, head, :, 0:128] = jnp.where(mine, part, 0.0).astype(jnp.bfloat16)
        value_ref[index, head, :, 128:256] = jnp.where(mine, jnp.broadcast_to(live, part.shape), 0.0).astype(jnp.bfloat16)


def attend(queries, key_at, value_at, bias_at):
    halves = []
    for group in range(HEADS // GROUP):
        q = queries[:, 128 * group:128 * (group + 1)]
        total = None
        for inner in range(GROUP):
            head = group * GROUP + inner
            scores = dot(q, key_at(head), NT)
            if bias_at is not None:
                scores = scores + bias_at(head)
            top = jnp.max(scores, axis=-1, keepdims=True)
            probs = jnp.exp2(scores - top).astype(jnp.bfloat16)
            product = dot(probs, value_at(head))
            total = product if total is None else total + product
        halves.append(total[:, 0:128] / total[:, 128:256])
    return jnp.concatenate(halves, axis=1)


def row_kernel(
    state_ref, token_ref, mask_ref, bias_ref, table_ref,
    wq_ref, wk_ref, wv_ref, wg_ref, wo_ref,
    out_ref,
    embedded_ref, query_ref, key_ref, value_ref, gate_ref, wide_ref,
):
    sequences, residues, channels = state_ref.shape
    peers, _, rows_each, _ = bias_ref.shape

    @pl.loop(0, sequences)
    def _(s):
        tokens = token_ref[pl.ds(s, 1), :]
        kinds = lax.broadcasted_iota(jnp.int32, (TOKEN_KINDS, residues), 0)
        indicator = (kinds == tokens).astype(jnp.float32).astype(jnp.bfloat16)
        embedded = state_ref[s].astype(jnp.float32) + dot(indicator, table_ref[...], TN)
        embedded_ref[s] = embedded
        normed = normalize(embedded).astype(jnp.bfloat16)
        query_ref[s] = (dot(normed, wq_ref[...]) * (HEAD_DIM ** -0.5 * LOG2E)).astype(jnp.bfloat16)
        store_keys(key_ref, s, dot(normed, wk_ref[...]))
        store_values(value_ref, s, dot(normed, wv_ref[...]), jnp.ones((1, 1), jnp.float32))
        gate_ref[s] = sigmoid(dot(normed, wg_ref[...])).astype(jnp.bfloat16)

    live = mask_ref[...] > 0
    blocks = QUERY_ROWS // rows_each

    @pl.loop(0, residues // QUERY_ROWS)
    def _(chunk):
        for head in range(HEADS):
            part = bias_ref[pl.ds(chunk * blocks, blocks), head].reshape(QUERY_ROWS, residues)
            wide_ref[head] = jnp.where(live, part.astype(jnp.float32) * LOG2E, MASKED)

        @pl.loop(0, sequences)
        def _(s):
            rows = pl.ds(pl.multiple_of(chunk * QUERY_ROWS, QUERY_ROWS), QUERY_ROWS)
            attended = attend(
                query_ref[s, rows, :],
                lambda head: key_ref[s, head],
                lambda head: value_ref[s, head],
                lambda head: wide_ref[head],
            )
            mixed = (attended * gate_ref[s, rows, :].astype(jnp.float32)).astype(jnp.bfloat16)
            updated = (embedded_ref[s, rows, :] + dot(mixed, wo_ref[...])).astype(jnp.bfloat16)
            out_ref[pl.ds(chunk * blocks, blocks), s] = updated.reshape(blocks, rows_each, channels)


def row_attention(state, tokens, mask, bias, table, weights):
    sequences, residues, channels = state.shape
    peers, _, rows_each, _ = bias.shape
    return pl.pallas_call(
        row_kernel,
        out_shape=jax.ShapeDtypeStruct((peers, sequences, rows_each, channels), jnp.bfloat16),
        in_specs=[pl.BlockSpec(memory_space=pltpu.VMEM)] * 10,
        out_specs=pl.BlockSpec(memory_space=pltpu.VMEM),
        scratch_shapes=[
            pltpu.VMEM((sequences, residues, channels), jnp.float32),
            pltpu.VMEM((sequences, residues, channels), jnp.bfloat16),
            pltpu.VMEM((sequences, HEADS, residues, 128), jnp.bfloat16),
            pltpu.VMEM((sequences, HEADS, residues, 256), jnp.bfloat16),
            pltpu.VMEM((sequences, residues, channels), jnp.bfloat16),
            pltpu.VMEM((HEADS, QUERY_ROWS, residues), jnp.float32),
        ],
        compiler_params=pltpu.CompilerParams(vmem_limit_bytes=VMEM_LIMIT),
        name="row_attention",
    )(state, tokens, mask, bias, table, *weights)


def column_kernel(
    arrived_ref, mask_ref, wq_ref, wk_ref, wv_ref, wg_ref, wo_ref,
    out_ref,
    wide_ref, key_ref, value_ref,
):
    sequences, residues, channels = arrived_ref.shape
    halves = 8

    @pl.loop(0, halves)
    def _(i):
        rows = sequences // halves
        part = arrived_ref[pl.ds(pl.multiple_of(i * rows, rows), rows)]
        part = part.astype(jnp.float32).reshape(rows * residues, channels)
        for half in range(2):
            wide_ref[half, pl.ds(pl.multiple_of(i * rows * residues, rows * residues), rows * residues), :] = (
                part[:, 128 * half:128 * (half + 1)]
            )

    live = jnp.transpose(jnp.broadcast_to(mask_ref[...].astype(jnp.float32), (128, sequences)))
    live = jnp.concatenate([live, live], axis=1)

    @pl.loop(0, residues)
    def _(r):
        updated = jnp.concatenate(
            [wide_ref[half, pl.ds(r, sequences, stride=residues), :] for half in range(2)], axis=1
        )
        normed = normalize(updated).astype(jnp.bfloat16)
        queries = (dot(normed, wq_ref[...]) * (HEAD_DIM ** -0.5 * LOG2E)).astype(jnp.bfloat16)
        keyed = dot(normed, wk_ref[...])
        keyed = jnp.where(live > 0.0, keyed, keyed[0:1, :])
        store_keys(key_ref, 0, keyed)
        store_values(value_ref, 0, dot(normed, wv_ref[...]) * live, live[:, 0:128])
        gate = sigmoid(dot(normed, wg_ref[...]))
        attended = attend(
            queries, lambda head: key_ref[0, head], lambda head: value_ref[0, head], None
        )
        mixed = (attended * gate).astype(jnp.bfloat16)
        result = updated + dot(mixed, wo_ref[...])
        for half in range(2):
            wide_ref[half, pl.ds(r, sequences, stride=residues), :] = result[:, 128 * half:128 * (half + 1)]

    @pl.loop(0, halves)
    def _(i):
        rows = sequences // halves
        span = pl.ds(pl.multiple_of(i * rows * residues, rows * residues), rows * residues)
        part = jnp.concatenate([wide_ref[half, span, :] for half in range(2)], axis=1)
        out_ref[pl.ds(pl.multiple_of(i * rows, rows), rows)] = (
            part.astype(jnp.bfloat16).reshape(rows, residues, channels)
        )


def column_attention(arrived, mask, weights):
    sequences, residues, channels = arrived.shape
    return pl.pallas_call(
        column_kernel,
        out_shape=jax.ShapeDtypeStruct(arrived.shape, jnp.bfloat16),
        in_specs=[pl.BlockSpec(memory_space=pltpu.VMEM)] * 7,
        out_specs=pl.BlockSpec(memory_space=pltpu.VMEM),
        scratch_shapes=[
            pltpu.VMEM((2, sequences * residues, 128), jnp.float32),
            pltpu.VMEM((1, HEADS, sequences, 128), jnp.bfloat16),
            pltpu.VMEM((1, HEADS, sequences, 256), jnp.bfloat16),
        ],
        compiler_params=pltpu.CompilerParams(vmem_limit_bytes=VMEM_LIMIT),
        name="column_attention",
    )(arrived, mask, *weights)


def body(
    alignment_state,
    token_index_grid,
    sequence_mask,
    residue_mask,
    pair_state,
    token_embedding_table,
    pair_bias_weight,
    row_query_weight,
    row_key_weight,
    row_value_weight,
    row_gate_weight,
    row_output_weight,
    column_query_weight,
    column_key_weight,
    column_value_weight,
    column_gate_weight,
    column_output_weight,
):
    bias_local = pair_bias(pair_state, pair_bias_weight)
    bias = lax.all_gather(bias_local, "dap", axis=0)
    blocks = row_attention(
        alignment_state, token_index_grid, residue_mask[None, :], bias, token_embedding_table,
        (row_query_weight, row_key_weight, row_value_weight, row_gate_weight, row_output_weight),
    )
    arrived = lax.all_to_all(blocks, "dap", split_axis=0, concat_axis=0, tiled=True)
    peers, seqs, rows_each, channels = blocks.shape
    arrived = arrived.reshape(peers * seqs, rows_each, channels)
    return column_attention(
        arrived, sequence_mask[None, :],
        (column_query_weight, column_key_weight, column_value_weight, column_gate_weight,
         column_output_weight),
    )


def solution(mesh):
    split = P(("dp", "dap"), None, None)
    in_specs = (
        split, P(("dp", "dap"), None), P("dp"), P("dp"), split,
    ) + (P(),) * 12
    return jax.shard_map(
        body, mesh=mesh, in_specs=in_specs, out_specs=P("dp", "dap", None), check_vma=False
    )
```

time: 357 us -> 220 us (0.62)
  matrix products: 165 us -> 0 us
  Pallas kernels: 0 us -> 87.3 us
  other arithmetic: 39.8 us -> 0 us
  blocking collectives: 0 us -> 32.9 us
  local copies, waits for them, and re-layouts: 31.2 us -> 1.39 us
  waiting for transfers between devices: 100 us -> 85.2 us
  starting transfers between devices: 4.66 us -> 0.01 us
    pallas_call x0 -> x3, Pallas kernels: none -> 87.3 us  [the longest x1 49.4 us: row_attention(): pl.pallas_call(row_kernel, out_shape=jax.ShapeDtypeStruct((peers, sequenc...]
    dot_general x18 -> x0, matrix products: 87 us -> none  [the longest x8 44.8 us: attend_block(): jnp.einsum('bhqk,bkhd->bqhd', attn_probs, valued, preferred_element_type=...]
    sub x8 -> x0, matrix products: 78.5 us -> none  [attend_block(): attn_probs = jax.nn.softmax(scores, axis=-1).astype(jnp.bfloat16)]
    all_to_all x0 -> x1, blocking collectives: none -> 32.9 us  [body(): lax.all_to_all(blocks, 'dap', split_axis=0, concat_axis=0, tiled=True)]
    all_to_all x1 -> x0, waiting for transfers between devices: 27 us -> none  [body(): lax.all_to_all(blocks, 'dap', split_axis=1, concat_axis=0, tiled=True)]
    convert_element_type x5 -> x0, other arithmetic: 26.8 us -> none  [the longest x4 26.3 us: attend_block(): scores = scores + bias_rows[None].astype(jnp.float32)]
    reduce_sum x5 -> x0, other arithmetic: 12.9 us -> none  [the longest x3 8.16 us: normalize(): variance = jnp.mean(centered * centered, axis=-1, keepdims=True)]
    reshape x3 -> x0, local copies, waits for them, and re-layouts: 12.4 us -> none  [the longest x2 10.8 us: grouped_attend(): return results.reshape((count,) + results.shape[2:])]
  transfers between devices with their start and end apart: 2 -> 1, of which waited for: 2 -> 1; matrix products, arithmetic and copies ran while one was open for 3% -> 0% of each run, Pallas kernels for 0% -> 0%
where the time goes in v1:
time: 220 us
  Pallas kernels  87.3 us (40%)
  waiting for transfers between devices  85.2 us (39%)
  blocking collectives  32.9 us (15%)
  between operations  13.4 us (6%)
    all_gather x1, waiting for transfers between devices, body(): bias = lax.all_gather(bias_local, 'dap', axis=0)  85.2 us
    pallas_call x1, Pallas kernels, row_attention(): pl.pallas_call(row_kernel, out_shape=jax.ShapeDtypeStruct((peers, sequenc...  49.4 us
    all_to_all x1, blocking collectives, body(): lax.all_to_all(blocks, 'dap', split_axis=0, concat_axis=0, tiled=True)  32.9 us
    pallas_call x1, Pallas kernels, column_attention(): pl.pallas_call(column_kernel, out_shape=jax.ShapeDtypeStruct(arrived.shap...  30.4 us
    pallas_call x1, Pallas kernels, pair_bias(): pl.pallas_call(bias_kernel, out_shape=jax.ShapeDtypeStruct((HEADS, rows,...  7.45 us
  transfers between devices with their start and end apart: 1, of which 1 were waited for; matrix products, arithmetic and copies ran while one was open for 0% of the time, Pallas kernels for 0%

profile of v1, /device:TPU:0, one launch (start us, length us, event | category | flops | bytes accessed | tf_op | source)
XLA Modules:
  0.0 220.2 jit_solution(2624491017451350222)
XLA Ops:
  6.5 0.0 all-gather.3.cloned.1.call-start
  6.5 1.4 copy.19.weight_ref
  7.9 7.5 %pair_bias.1 = bf16[8,16,512]{2,1,0:T(8,128)(2,1)} custom-call(bf16[16,512,128]{2,1,0:T(8,128)(2,1)} %pair_ref.1, bf16[128,8]{1,0:T(8,128)(2,1)} %copy.19.weight_ref), custom_call_target="tpu_custom_call" | custom-call | tf_op jit(solution)/shard_map/pair_bias/pallas_call | solution.py:58
  15.4 0.0 all-gather.3.cloned.1.call-update
  15.4 85.2 %all-gather.3.cloned.1.call-done = bf16[256,16,512]{2,1,0:T(8,128)(2,1)} async-done(((bf16[8,16,512]{2,1,0:T(8,128)(2,1)}), bf16[256,16,512]{2,1,0:T(8,128)(2,1)}) %all-gather.3.cloned.1.call-update) | async-done | bytes 4194320 | tf_op jit(solution)/shard_map/all_gather | solution.py:256
  100.6 49.4 %row_attention.1 = bf16[32,8,16,256]{3,2,1,0:T(8,128)(2,1)} custom-call(bf16[8,512,256]{2,1,0:T(8,128)(2,1)} %state_ref.1, s32[8,512]{1,0:T(8,128)} %token_ref.1, s32[1,512]{1,0:T(1,128)} %bitcast.6, bf16[32,8,16,512]{3,2,1,0:T(8,128)(2,1)} %bitcast.5, bf16[23,256]{1,0:T(8,128)(2,1)} %table_ref.1, bf16[256,256]{1,0:T(8,128)(2,1)} %wq_ref.2, ...), custom_call_target="tpu_custom_call" | custom-call | tf_op jit(solution)/shard_map/row_attention/pallas_call | solution.py:150
  150.0 32.9 %all_to_all.5 = bf16[32,8,16,256]{3,2,1,0:T(8,128)(2,1)} all-to-all(bf16[32,8,16,256]{3,2,1,0:T(8,128)(2,1)} %row_attention.1), channel_id=1, replica_groups=mesh['dp'=4,'dap'=32] {'dap'}, dimensions={0} | all-to-all | bytes 4194304 | tf_op jit(solution)/shard_map/all_to_all | solution.py:261
  182.9 30.4 %column_attention.1 = bf16[256,16,256]{2,1,0:T(8,128)(2,1)} custom-call(bf16[256,16,256]{2,1,0:T(8,128)(2,1)} %bitcast.4, s32[1,256]{1,0:T(1,128)} %bitcast.7, bf16[256,256]{1,0:T(8,128)(2,1)} %wq_ref.3, bf16[256,256]{1,0:T(8,128)(2,1)} %wk_ref.3, bf16[256,256]{1,0:T(8,128)(2,1)} %wv_ref.3, bf16[256,256]{1,0:T(8,128)(2,1)} %wg_ref.3, bf16[256,256]{1,0:T(8,128)(2,1)} %wo_ref.3), custom_call_target="tpu_custom_call" | custom-call | tf_op jit(solution)/shard_map/column_attention/pallas_call | solution.py:221
Async XLA Ops:
  6.5 94.1 %all-gather.3.cloned.1.call-start = ((), (), s32[]{:S(2)}) async-start(), calls=%async_computation.1 | async-start | bytes 4325376 | tf_op jit(solution)/shard_map/all_gather | solution.py:256
Sparse Core Ops, SparseCore 0:
  15.5 85.0 all-gather.2

commit v2 on v1

--- a/solution.py
+++ b/solution.py
@@ -15,6 +15,9 @@
 LOG2E = 1.4426950408889634
 MASKED = -1e9
 QUERY_ROWS = 128
+PIECE = 4
+XS, ZS, YS = 4, 2, 4
+MESH = pl.DeviceIdType.MESH
 VMEM_LIMIT = 60 * 1024 * 1024
 
 NT = (((1,), (1,)), ((), ()))
@@ -37,32 +40,6 @@
 
 def lane_head(shape):
     return lax.broadcasted_iota(jnp.int32, shape, len(shape) - 1) // HEAD_DIM
-
-
-def bias_kernel(pair_ref, weight_ref, out_ref):
-    rows = pair_ref.shape[0]
-    channels = pair_ref.shape[2]
-    weight = weight_ref[...]
-    averaging = jnp.full((channels, channels), 1.0 / channels, jnp.bfloat16)
-    for row in range(rows):
-        block = pair_ref[row]
-        centered = block.astype(jnp.float32) - dot(block, averaging)
-        variance = dot((centered * centered).astype(jnp.bfloat16), averaging)
-        normed = (centered * lax.rsqrt(variance + EPSILON)).astype(jnp.bfloat16)
-        projected = dot(weight, normed, (((0,), (1,)), ((), ())))
-        out_ref[:, row, :] = projected.astype(jnp.bfloat16)
-
-
-def pair_bias(pair_state, weight):
-    rows, keys, channels = pair_state.shape
-    return pl.pallas_call(
-        bias_kernel,
-        out_shape=jax.ShapeDtypeStruct((HEADS, rows, keys), jnp.bfloat16),
-        in_specs=[pl.BlockSpec(memory_space=pltpu.VMEM)] * 2,
-        out_specs=pl.BlockSpec(memory_space=pltpu.VMEM),
-        compiler_params=pltpu.CompilerParams(vmem_limit_bytes=VMEM_LIMIT),
-        name="pair_bias",
-    )(pair_state, weight)
 
 
 def store_keys(key_ref, index, keyed):
@@ -99,14 +76,127 @@
     return jnp.concatenate(halves, axis=1)
 
 
+def gather_plan():
+    def place(half, u, z, v):
+        return (v % XS, z % ZS, u % YS) if half == 0 else (u % XS, z % ZS, v % YS)
+
+    first, steps = [], []
+    for half in range(2):
+        own = place(half, 0, 0, 0)
+        for target in ((0, 1, 0), (1, 0, 0), (-1, 0, 0), (0, 0, 1), (0, 0, -1)):
+            first.append((half, own, place(half, *target)))
+        for u in (0, 1, -1, 2):
+            for z in range(2):
+                for v in (0, 1, -1, 2):
+                    if (u, z, v) == (0, 0, 0):
+                        continue
+                    block, to = place(half, u, z, v), []
+                    if v == 0:
+                        if u == 0:
+                            to += [(1, 0, 0), (-1, 0, 0)]
+                        if (u, z) == (-1, 0):
+                            to.append((1, 0, 0))
+                        if (u, z) == (1, 1):
+                            to.append((-1, 0, 0))
+                        to += [(0, 0, 1), (0, 0, -1)]
+                    if (z, v) == (0, -1):
+                        to.append((0, 0, 1))
+                    if (z, v) == (1, 1):
+                        to.append((0, 0, -1))
+                    hops = abs(u) + abs(v) + 1.5 * z
+                    rank = (0, 1, 3, 2)[block[0]]
+                    sends = [(half, block, place(half, *t)) for t in to]
+                    steps.append((hops + 0.5 * rank + (0 if sends else 0.75), rank, half, block, sends))
+    steps.sort(key=lambda step: step[:4])
+    return first, [(step[1], (step[2], step[3]), step[4]) for step in steps]
+
+
+def fill_slots(steps):
+    slots, place = {}, 0
+    room = [("project", s, 4) for s in range(8)]
+    room += [(chunk, s, 2) for chunk in range(2) for s in range(8)]
+    for stage, s, count in room:
+        taken = steps[place:place + count]
+        place += len(taken)
+        slots[stage, s] = taken
+    moved = {}
+    order = ["project", 0, 1, 2]
+    for chunk in range(3):
+        late = []
+        for (stage, s), taken in slots.items():
+            if order.index(stage) > chunk:
+                late += [step for step in taken if step[0] <= chunk]
+                slots[stage, s] = [step for step in taken if step[0] > chunk]
+        moved[chunk] = late
+    return slots, moved
+
+
 def row_kernel(
-    state_ref, token_ref, mask_ref, bias_ref, table_ref,
+    pair_ref, pair_weight_ref, state_ref, token_ref, mask_ref, table_ref,
     wq_ref, wk_ref, wv_ref, wg_ref, wo_ref,
-    out_ref,
-    embedded_ref, query_ref, key_ref, value_ref, gate_ref, wide_ref,
+    arrived_ref,
+    bias_ref, embedded_ref, query_ref, key_ref, value_ref, gate_ref, wide_ref, updated_ref,
+    gather_send, gather_recv, turn_send, turn_recv, own_sem,
 ):
     sequences, residues, channels = state_ref.shape
     peers, _, rows_each, _ = bias_ref.shape
+    me = lax.axis_index("dap")
+    x, z, y = me // (ZS * YS), (me // YS) % ZS, me % YS
+
+    def at(offset):
+        dx, dz, dy = offset
+        return (((x + dx) % XS) * ZS + (z + dz) % ZS) * YS + (y + dy) % YS
+
+    barrier = pltpu.get_barrier_semaphore()
+    for step in range(1, peers):
+        pl.semaphore_signal(
+            barrier, inc=1, device_id={"dap": (me + step) % peers}, device_id_type=MESH
+        )
+
+    pair_channels = pair_ref.shape[2]
+    averaging = jnp.full((pair_channels, pair_channels), 1.0 / pair_channels, jnp.bfloat16)
+    spread = jnp.transpose(pair_weight_ref[...].astype(jnp.float32))
+    spread = jnp.broadcast_to(spread[:, None, :], (HEADS, rows_each, pair_channels))
+    spread = spread.reshape(HEADS * rows_each, pair_channels)
+    row_of = lax.broadcasted_iota(jnp.int32, spread.shape, 0) % rows_each
+    total = None
+    for row in range(rows_each):
+        block = pair_ref[row]
+        centered = block.astype(jnp.float32) - dot(block, averaging)
+        variance = dot((centered * centered).astype(jnp.bfloat16), averaging)
+        normed = (centered * lax.rsqrt(variance + EPSILON)).astype(jnp.bfloat16)
+        weight = jnp.where(row_of == row, spread, 0.0).astype(jnp.bfloat16)
+        product = dot(weight, normed, NT)
+        total = product if total is None else total + product
+    bias_ref[me] = total.astype(jnp.bfloat16).reshape(HEADS, rows_each, residues)
+
+    pl.semaphore_wait(barrier, peers - 1)
+
+    first, steps = gather_plan()
+    sends = first + [send for step in steps for send in step[2]]
+    number = {send: i for i, send in enumerate(sends)}
+
+    def gather_copy(half, block, target, index):
+        part = bias_ref.at[block, pl.ds(half * (HEADS // 2), HEADS // 2)]
+        return pltpu.make_async_remote_copy(
+            src_ref=part, dst_ref=part,
+            send_sem=gather_send.at[index], recv_sem=gather_recv.at[half, block],
+            device_id={"dap": target}, device_id_type=MESH,
+        )
+
+    def start(send):
+        half, block, target = send
+        gather_copy(half, at(block), at(target), number[send]).start()
+
+    def run(steps):
+        for _, (half, block), sends in steps:
+            gather_copy(half, at(block), at((0, 1, 0)), 0).wait_recv()
+            for send in sends:
+                start(send)
+
+    for send in first:
+        start(send)
+    slots, moved = fill_slots(steps)
 
     @pl.loop(0, sequences)
     def _(s):
@@ -120,19 +210,41 @@
         store_keys(key_ref, s, dot(normed, wk_ref[...]))
         store_values(value_ref, s, dot(normed, wv_ref[...]), jnp.ones((1, 1), jnp.float32))
         gate_ref[s] = sigmoid(dot(normed, wg_ref[...])).astype(jnp.bfloat16)
+        for k in range(8):
+            if slots["project", k]:
+                pl.when(s == k)(functools.partial(run, slots["project", k]))
 
     live = mask_ref[...] > 0
     blocks = QUERY_ROWS // rows_each
 
-    @pl.loop(0, residues // QUERY_ROWS)
+    def turn_copy(target, slot, piece):
+        span = pl.ds(piece * PIECE, PIECE)
+        return pltpu.make_async_remote_copy(
+            src_ref=updated_ref.at[target, span], dst_ref=arrived_ref.at[slot, span],
+            send_sem=turn_send.at[target, piece], recv_sem=turn_recv.at[slot, piece],
+            device_id={"dap": target}, device_id_type=MESH,
+        )
+
+    def own_copy(piece):
+        span = pl.ds(piece * PIECE, PIECE)
+        return pltpu.make_async_copy(
+            updated_ref.at[me, span], arrived_ref.at[me, span], own_sem.at[piece]
+        )
+
+    @pl.loop(0, XS)
     def _(chunk):
+        far = (chunk * (chunk + 1) // 2) % XS
+        cx = (x + far) % XS
+        for k in range(3):
+            if moved[k]:
+                pl.when(chunk == k)(functools.partial(run, moved[k]))
         for head in range(HEADS):
-            part = bias_ref[pl.ds(chunk * blocks, blocks), head].reshape(QUERY_ROWS, residues)
+            part = bias_ref[pl.ds(cx * blocks, blocks), head].reshape(QUERY_ROWS, residues)
             wide_ref[head] = jnp.where(live, part.astype(jnp.float32) * LOG2E, MASKED)
 
         @pl.loop(0, sequences)
         def _(s):
-            rows = pl.ds(pl.multiple_of(chunk * QUERY_ROWS, QUERY_ROWS), QUERY_ROWS)
+            rows = pl.ds(pl.multiple_of(cx * QUERY_ROWS, QUERY_ROWS), QUERY_ROWS)
             attended = attend(
                 query_ref[s, rows, :],
                 lambda head: key_ref[s, head],
@@ -141,28 +253,73 @@
             )
             mixed = (attended * gate_ref[s, rows, :].astype(jnp.float32)).astype(jnp.bfloat16)
             updated = (embedded_ref[s, rows, :] + dot(mixed, wo_ref[...])).astype(jnp.bfloat16)
-            out_ref[pl.ds(chunk * blocks, blocks), s] = updated.reshape(blocks, rows_each, channels)
-
-
-def row_attention(state, tokens, mask, bias, table, weights):
+            updated_ref[pl.ds(cx * blocks, blocks), s] = updated.reshape(blocks, rows_each, channels)
+            for c in range(2):
+                for k in range(8):
+                    if slots[c, k]:
+                        pl.when((chunk == c) & (s == k))(functools.partial(run, slots[c, k]))
+
+            @pl.when(s % PIECE == PIECE - 1)
+            def _():
+                piece = s // PIECE
+                for j in range(blocks):
+                    target = (cx * ZS + (z + j // YS) % ZS) * YS + (y + j) % YS
+                    if j == 0:
+                        @pl.when(chunk == 0)
+                        def _():
+                            own_copy(piece).start()
+
+                        @pl.when(chunk > 0)
+                        def _():
+                            turn_copy(target, me, piece).start()
+                    else:
+                        turn_copy(target, me, piece).start()
+
+    for send in sends:
+        half, block, target = send
+        gather_copy(half, at(block), at(target), number[send]).wait_send()
+
+    @pl.loop(1, peers)
+    def _(step):
+        other = (me + step) % peers
+        for piece in range(sequences // PIECE):
+            turn_copy(other, other, piece).wait_send()
+            turn_copy(other, other, piece).wait_recv()
+
+    for piece in range(sequences // PIECE):
+        own_copy(piece).wait()
+
+
+def row_attention(pair_state, pair_weight, state, tokens, mask, table, weights):
     sequences, residues, channels = state.shape
-    peers, _, rows_each, _ = bias.shape
+    rows_each = pair_state.shape[0]
+    peers = XS * ZS * YS
+    block = (peers, sequences, rows_each, channels)
     return pl.pallas_call(
         row_kernel,
-        out_shape=jax.ShapeDtypeStruct((peers, sequences, rows_each, channels), jnp.bfloat16),
-        in_specs=[pl.BlockSpec(memory_space=pltpu.VMEM)] * 10,
-        out_specs=pl.BlockSpec(memory_space=pltpu.VMEM),
+        out_shape=jax.ShapeDtypeStruct(block, jnp.bfloat16),
+        in_specs=[pl.BlockSpec(memory_space=pltpu.VMEM)] * 11,
+        out_specs=pl.BlockSpec(memory_space=pl.ANY),
         scratch_shapes=[
+            pltpu.VMEM((peers, HEADS, rows_each, residues), jnp.bfloat16),
             pltpu.VMEM((sequences, residues, channels), jnp.float32),
             pltpu.VMEM((sequences, residues, channels), jnp.bfloat16),
             pltpu.VMEM((sequences, HEADS, residues, 128), jnp.bfloat16),
             pltpu.VMEM((sequences, HEADS, residues, 256), jnp.bfloat16),
             pltpu.VMEM((sequences, residues, channels), jnp.bfloat16),
             pltpu.VMEM((HEADS, QUERY_ROWS, residues), jnp.float32),
+            pltpu.VMEM(block, jnp.bfloat16),
+            pltpu.SemaphoreType.DMA((62,)),
+            pltpu.SemaphoreType.DMA((2, peers)),
+            pltpu.SemaphoreType.DMA((peers, sequences // PIECE)),
+            pltpu.SemaphoreType.DMA((peers, sequences // PIECE)),
+            pltpu.SemaphoreType.DMA((sequences // PIECE,)),
         ],
-        compiler_params=pltpu.CompilerParams(vmem_limit_bytes=VMEM_LIMIT),
+        compiler_params=pltpu.CompilerParams(
+            vmem_limit_bytes=VMEM_LIMIT, collective_id=0, has_side_effects=True
+        ),
         name="row_attention",
-    )(state, tokens, mask, bias, table, *weights)
+    )(pair_state, pair_weight, state, tokens, mask, table, *weights)
 
 
 def column_kernel(
@@ -252,14 +409,12 @@
     column_gate_weight,
     column_output_weight,
 ):
-    bias_local = pair_bias(pair_state, pair_bias_weight)
-    bias = lax.all_gather(bias_local, "dap", axis=0)
-    blocks = row_attention(
-        alignment_state, token_index_grid, residue_mask[None, :], bias, token_embedding_table,
+    arrived = row_attention(
+        pair_state, pair_bias_weight, alignment_state, token_index_grid, residue_mask[None, :],
+        token_embedding_table,
         (row_query_weight, row_key_weight, row_value_weight, row_gate_weight, row_output_weight),
     )
-    arrived = lax.all_to_all(blocks, "dap", split_axis=0, concat_axis=0, tiled=True)
-    peers, seqs, rows_each, channels = blocks.shape
+    peers, seqs, rows_each, channels = arrived.shape
     arrived = arrived.reshape(peers * seqs, rows_each, channels)
     return column_attention(
         arrived, sequence_mask[None, :],

time: 220 us -> 117 us (0.53)
  waiting for transfers between devices: 85.2 us -> 0 us
  blocking collectives: 32.9 us -> 0 us
  Pallas kernels: 87.3 us -> 115 us
  between operations: 13.4 us -> 0.01 us
    all_gather x1 -> x0, waiting for transfers between devices: 85.2 us -> none  [body(): bias = lax.all_gather(bias_local, 'dap', axis=0)]
    all_to_all x1 -> x0, blocking collectives: 32.9 us -> none  [body(): lax.all_to_all(blocks, 'dap', split_axis=0, concat_axis=0, tiled=True)]
    pallas_call x2 -> x1, Pallas kernels: 56.9 us -> 84.8 us  [row_attention(): pl.pallas_call(row_kernel, out_shape=jax.ShapeDtypeStruct(block, jnp.bflo...]
  transfers between devices with their start and end apart: 1 -> 0, of which waited for: 1 -> 0; matrix products, arithmetic and copies ran while one was open for 0% -> 0% of each run, Pallas kernels for 0% -> 0%
where the time goes in v2:
time: 117 us
  Pallas kernels  115 us (98%)
  local copies, waits for them, and re-layouts  1.4 us (1%)
    pallas_call x1, Pallas kernels, row_attention(): pl.pallas_call(row_kernel, out_shape=jax.ShapeDtypeStruct(block, jnp.bflo...  84.8 us
    pallas_call x1, Pallas kernels, column_attention(): pl.pallas_call(column_kernel, out_shape=jax.ShapeDtypeStruct(arrived.shap...  30.4 us

profile of v2, /device:TPU:0, one launch (start us, length us, event | category | flops | bytes accessed | tf_op | source)
XLA Modules:
  0.0 116.6 jit_solution(10347826610638942957)
XLA Ops:
  0.0 1.4 %copy.18.pair_weight_ref = bf16[128,8]{1,0:T(8,128)(2,1)} copy(bf16[128,8]{0,1:T(8,128)(2,1)} %param.23) | data formatting | bytes 4096 | tf_op args[6]
  1.4 84.8 %row_attention.1 = bf16[32,8,16,256]{3,2,1,0:T(8,128)(2,1)} custom-call(bf16[16,512,128]{2,1,0:T(8,128)(2,1)} %pair_ref.1, bf16[128,8]{1,0:T(8,128)(2,1)} %copy.18.pair_weight_ref, bf16[8,512,256]{2,1,0:T(8,128)(2,1)} %state_ref.1, s32[8,512]{1,0:T(8,128)} %token_ref.1, s32[1,512]{1,0:T(1,128)} %bitcast.4, bf16[23,256]{1,0:T(8,128)(2,1)} %table_ref.1, ...), custom_call_target="tpu_custom_call" | custom-call | tf_op jit(solution)/shard_map/row_attention/pallas_call | solution.py:298
  86.2 30.4 %column_attention.1 = bf16[256,16,256]{2,1,0:T(8,128)(2,1)} custom-call(bf16[256,16,256]{2,1,0:T(8,128)(2,1)} %bitcast.3, s32[1,256]{1,0:T(1,128)} %bitcast.5, bf16[256,256]{1,0:T(8,128)(2,1)} %wq_ref.3, bf16[256,256]{1,0:T(8,128)(2,1)} %wk_ref.3, bf16[256,256]{1,0:T(8,128)(2,1)} %wv_ref.3, bf16[256,256]{1,0:T(8,128)(2,1)} %wg_ref.3, bf16[256,256]{1,0:T(8,128)(2,1)} %wo_ref.3), custom_call_target="tpu_custom_call" | custom-call | tf_op jit(solution)/shard_map/column_attention/pallas_call | solution.py:378

commit v3 on v0

v3 whole, which is shorter than its diff:
```python
import functools

import jax
import jax.numpy as jnp
from jax import lax
from jax.experimental import pallas as pl
from jax.experimental.pallas import tpu as pltpu
from jax.sharding import PartitionSpec as P

HEADS = 8
HEAD_DIM = 32
GROUP = 4
TOKEN_KINDS = 23
EPSILON = 1e-05
LOG2E = 1.4426950408889634
MASKED = -1e9
ROWS = 8
PIECE = 2
COLUMNS = 2
LATER = 2.5
PROJECT_STEPS = (6, 8, 8, 8, 8, 8, 8, 8)
ATTEND_STEPS = (20, 20, 22, 0)
XS, ZS, YS = 4, 2, 4
MESH = pl.DeviceIdType.MESH
VMEM_LIMIT = 60 * 1024 * 1024

NT = (((1,), (1,)), ((), ()))
TN = (((0,), (0,)), ((), ()))


def dot(a, b, dims=(((1,), (0,)), ((), ()))):
    return lax.dot_general(a, b, dims, preferred_element_type=jnp.float32)


def normalize(values):
    centered = values - jnp.mean(values, axis=-1, keepdims=True)
    variance = jnp.mean(centered * centered, axis=-1, keepdims=True)
    return centered * lax.rsqrt(variance + EPSILON)


def sigmoid(x):
    return 0.5 * jnp.tanh(0.5 * x) + 0.5


def lane_head(shape):
    return lax.broadcasted_iota(jnp.int32, shape, len(shape) - 1) // HEAD_DIM


def head_lanes(inner):
    return (lane_head((1, 128)) == inner).astype(jnp.float32).astype(jnp.bfloat16)


def attend(queries, key_at, value_at, ones_at, bias_at):
    halves = []
    for group in range(HEADS // GROUP):
        q = queries[:, 128 * group:128 * (group + 1)]
        keyed, valued = key_at(group), value_at(group)
        all_probs, all_values = [], []
        for inner in range(GROUP):
            mine = head_lanes(inner)
            scores = dot(q, keyed * mine, NT)
            if bias_at is not None:
                scores = scores + bias_at(group * GROUP + inner)
            top = jnp.max(scores, axis=-1, keepdims=True)
            all_probs.append(jnp.exp2(scores - top).astype(jnp.bfloat16))
            all_values.append(jnp.concatenate([valued * mine, ones_at(inner)], axis=1))
        total = dot(jnp.concatenate(all_probs, axis=1), jnp.concatenate(all_values, axis=0))
        halves.append(total[:, 0:128] / total[:, 128:256])
    return jnp.concatenate(halves, axis=1)


def gather_plan():
    def place(half, u, z, v):
        return (v % XS, z % ZS, u % YS) if half == 0 else (u % XS, z % ZS, v % YS)

    first, steps = [], []
    for rows in range(2):
        for half in range(2):
            part = (rows, half)
            for target in ((0, 1, 0), (1, 0, 0), (-1, 0, 0), (0, 0, 1), (0, 0, -1)):
                first.append((part, (0, 0, 0), place(half, *target)))
            for u in (0, 1, -1, 2):
                for z in range(2):
                    for v in (0, 1, -1, 2):
                        if (u, z, v) == (0, 0, 0):
                            continue
                        to = []
                        if v == 0:
                            if u == 0:
                                to += [(1, 0, 0), (-1, 0, 0)]
                            if (u, z) == (-1, 0):
                                to.append((1, 0, 0))
                            if (u, z) == (1, 1):
                                to.append((-1, 0, 0))
                            to += [(0, 0, 1), (0, 0, -1)]
                        if (z, v) == (0, -1):
                            to.append((0, 0, 1))
                        if (z, v) == (1, 1):
                            to.append((0, 0, -1))
                        hops = abs(u) + abs(v) + 1.5 * z
                        order = hops + LATER * rows + (0 if to else 0.75)
                        steps.append((order, part, place(half, u, z, v), [place(half, *t) for t in to]))
    steps.sort(key=lambda step: step[:3])
    return first, [step[1:] for step in steps]


def fill_slots(steps):
    slots, place = {}, 0
    room = [("project", s, n) for s, n in enumerate(PROJECT_STEPS)]
    room += [("attend", s, n) for s, n in enumerate(ATTEND_STEPS)]
    for stage, s, count in room:
        slots[stage, s] = steps[place:place + count]
        place += count
    rest = steps[place:]
    early = []
    for (stage, s), taken in slots.items():
        if stage == "attend":
            early += [step for step in taken if step[0][0] == 0]
            slots[stage, s] = [step for step in taken if step[0][0] == 1]
    early += [step for step in rest if step[0][0] == 0]
    return slots, early, [step for step in rest if step[0][0] == 1]


def kernel(
    pair_ref, pair_weight_ref, state_ref, token_ref, residue_mask_ref, sequence_mask_ref, table_ref,
    row_wq, row_wk, row_wv, row_wg, row_wo, col_wq, col_wk, col_wv, col_wg, col_wo,
    out_ref,
    local_ref, bias_ref, embedded_ref, query_ref, key_ref, value_ref, gate_ref, wide_ref,
    updated_ref, arrived_ref, col_query, col_key, col_value, col_gate, live_ref, result_ref,
    local_sem, gather_send, gather_recv, turn_send, turn_recv,
):
    sequences, residues, channels = local_ref.shape
    rows_each, _, pair_channels = pair_ref.shape
    peers = residues // rows_each
    me = lax.axis_index("dap")
    x, z, y = me // (ZS * YS), (me // YS) % ZS, me % YS

    def at(offset):
        dx, dz, dy = offset
        return (((x + dx) % XS) * ZS + (z + dz) % ZS) * YS + (y + dy) % YS

    load = pltpu.make_async_copy(state_ref, local_ref, local_sem)
    load.start()
    barrier = pltpu.get_barrier_semaphore()
    for step in range(1, peers):
        pl.semaphore_signal(
            barrier, inc=1, device_id={"dap": (me + step) % peers}, device_id_type=MESH
        )

    first, steps = gather_plan()
    sends = first + [(part, block, target) for part, block, to in steps for target in to]
    number = {send: i for i, send in enumerate(sends)}

    def gather_copy(part, block, target, index):
        rows, half = part
        piece = bias_ref.at[rows, block, pl.ds(half * (HEADS // 2) * ROWS, HEADS // 2 * ROWS)]
        return pltpu.make_async_remote_copy(
            src_ref=piece, dst_ref=piece,
            send_sem=gather_send.at[index], recv_sem=gather_recv.at[rows, half, block],
            device_id={"dap": target}, device_id_type=MESH,
        )

    def start(send):
        part, block, target = send
        gather_copy(part, at(block), at(target), number[send]).start()

    def run(steps):
        for part, block, to in steps:
            gather_copy(part, at(block), at((0, 1, 0)), 0).wait_recv()
            for target in to:
                start((part, block, target))

    averaging = jnp.full((pair_channels, pair_channels), 1.0 / pair_channels, jnp.bfloat16)
    spread = pair_weight_ref[...].astype(jnp.float32)
    spread = jnp.broadcast_to(spread[:, None, :], (HEADS, ROWS, pair_channels))
    spread = spread.reshape(HEADS * ROWS, pair_channels)
    row_of = lax.broadcasted_iota(jnp.int32, spread.shape, 0) % ROWS
    for rows in range(2):
        total = None
        for row in range(ROWS):
            block = pair_ref[rows * ROWS + row]
            centered = block.astype(jnp.float32) - dot(block, averaging)
            variance = dot((centered * centered).astype(jnp.bfloat16), averaging)
            normed = (centered * lax.rsqrt(variance + EPSILON)).astype(jnp.bfloat16)
            weight = jnp.where(row_of == row, spread, 0.0).astype(jnp.bfloat16)
            product = dot(weight, normed, NT)
            total = product if total is None else total + product
        bias_ref[rows, me] = total.astype(jnp.bfloat16)
        if rows == 0:
            pl.semaphore_wait(barrier, peers - 1)
        for send in first:
            if send[0][0] == rows:
                start(send)

    slots, early, rest = fill_slots(steps)
    load.wait()

    def by_half(values):
        return jnp.swapaxes(values.reshape(peers, 2, ROWS, channels), 0, 1).reshape(
            2, peers * ROWS, channels
        )

    @pl.loop(0, sequences)
    def _(s):
        tokens = token_ref[pl.ds(s, 1), :]
        kinds = lax.broadcasted_iota(jnp.int32, (TOKEN_KINDS, residues), 0)
        indicator = (kinds == tokens).astype(jnp.float32).astype(jnp.bfloat16)
        embedded = local_ref[s].astype(jnp.float32) + dot(indicator, table_ref[...], TN)
        embedded_ref[s] = by_half(embedded)
        normed = normalize(embedded).astype(jnp.bfloat16)
        queries = dot(normed, row_wq[...]) * (HEAD_DIM ** -0.5 * LOG2E)
        query_ref[s] = by_half(queries).astype(jnp.bfloat16)
        key_ref[s] = dot(normed, row_wk[...]).astype(jnp.bfloat16)
        value_ref[s] = dot(normed, row_wv[...]).astype(jnp.bfloat16)
        gate_ref[s] = by_half(sigmoid(dot(normed, row_wg[...]))).astype(jnp.bfloat16)
        for k in range(sequences):
            if slots["project", k]:
                pl.when(s == k)(functools.partial(run, slots["project", k]))

    real = residue_mask_ref[...] > 0
    pairs = sequences // 2
    pieces = pairs // PIECE

    def turn_copy(rows, target, slot, piece):
        span = pl.ds(piece * PIECE, PIECE)
        return pltpu.make_async_remote_copy(
            src_ref=updated_ref.at[rows, target, span], dst_ref=arrived_ref.at[rows, slot, span],
            send_sem=turn_send.at[rows, target, piece], recv_sem=turn_recv.at[rows, slot, piece],
            device_id={"dap": target}, device_id_type=MESH,
        )

    run(early)

    @pl.loop(0, 2)
    def _(rows):
        if rest:
            pl.when(rows == 1)(functools.partial(run, rest))
        for head in range(0, HEADS, 2):
            both = bias_ref[rows, :, ROWS * head:ROWS * (head + 2), :].astype(jnp.float32) * LOG2E
            for i in range(2):
                part = both[:, ROWS * i:ROWS * (i + 1), :].reshape(peers * ROWS, residues)
                wide_ref[head + i] = jnp.where(real, part, MASKED)

        @pl.loop(0, pairs)
        def _(p):
            results = []
            for i in range(2):
                s = 2 * p + i
                attended = attend(
                    query_ref[s, rows],
                    lambda g: key_ref[s, :, 128 * g:128 * (g + 1)],
                    lambda g: value_ref[s, :, 128 * g:128 * (g + 1)],
                    lambda inner: jnp.broadcast_to(head_lanes(inner), (residues, 128)),
                    lambda head: wide_ref[head],
                )
                mixed = (attended * gate_ref[s, rows].astype(jnp.float32)).astype(jnp.bfloat16)
                updated = embedded_ref[s, rows] + dot(mixed, row_wo[...])
                results.append(updated.reshape(peers, ROWS, channels))
            updated_ref[rows, :, p] = jnp.concatenate(results, axis=1).astype(jnp.bfloat16)
            arrived_ref[rows, me, p] = updated_ref[rows, me, p]
            for k in range(pairs):
                if slots["attend", k]:
                    pl.when((rows == 0) & (p == k))(functools.partial(run, slots["attend", k]))

            @pl.when(p % PIECE == PIECE - 1)
            def _():
                for step in range(1, peers):
                    turn_copy(rows, (me + step) % peers, me, p // PIECE).start()

    tokens = 512
    lines = tokens // ROWS
    sources = lines // sequences
    everyone = peers * sequences
    real = jnp.broadcast_to(sequence_mask_ref[...].astype(jnp.float32), (128, everyone))
    real = jnp.transpose(real)
    for inner in range(GROUP):
        live_ref[inner] = real.astype(jnp.bfloat16) * head_lanes(inner)
    real = jnp.concatenate([real, real], axis=1)

    for rows in range(2):
        def arrivals(i):
            part = arrived_ref[rows, pl.ds(i * sources, sources)]
            return part.astype(jnp.float32).reshape(tokens, channels)

        def span_of(i):
            return pl.ds(pl.multiple_of(i * tokens, tokens), tokens)

        @pl.loop(0, peers // sources)
        def _(i):
            for j in range(sources):
                source = i * sources + j

                @pl.when(source != me)
                def _():
                    for piece in range(pieces):
                        turn_copy(rows, source, source, piece).wait_recv()
            span = span_of(i)
            normed = normalize(arrivals(i)).astype(jnp.bfloat16)
            queries = dot(normed, col_wq[...]) * (HEAD_DIM ** -0.5 * LOG2E)
            keyed = dot(normed, col_wk[...])
            valued = dot(normed, col_wv[...])
            for half in range(2):
                lanes = slice(128 * half, 128 * (half + 1))
                col_query[half, span, :] = queries[:, lanes]
                col_key[half, span, :] = keyed[:, lanes]
                col_value[half, span, :] = valued[:, lanes]
            col_gate[span, :] = sigmoid(dot(normed, col_wg[...])).astype(jnp.bfloat16)

        @pl.loop(0, ROWS // COLUMNS)
        def _(i):
            spans = [pl.ds(i * COLUMNS + j, everyone, stride=ROWS) for j in range(COLUMNS)]

            def line(ref, span):
                return jnp.concatenate([ref[half, span, :] for half in range(2)], axis=1)

            loaded = [[line(ref, span) for ref in (col_query, col_key, col_value)] for span in spans]
            results = []
            for queries, keyed, valued in loaded:
                keyed = jnp.where(real > 0.0, keyed, keyed[0:1, :]).astype(jnp.bfloat16)
                valued = (valued * real).astype(jnp.bfloat16)
                results.append(attend(
                    queries.astype(jnp.bfloat16),
                    lambda g: keyed[:, 128 * g:128 * (g + 1)],
                    lambda g: valued[:, 128 * g:128 * (g + 1)],
                    lambda inner: live_ref[inner],
                    None,
                ))
            for span, attended in zip(spans, results):
                for half in range(2):
                    col_query[half, span, :] = attended[:, 128 * half:128 * (half + 1)]

        @pl.loop(0, peers // sources)
        def _(i):
            span = span_of(i)
            attended = jnp.concatenate([col_query[half, span, :] for half in range(2)], axis=1)
            mixed = (attended * col_gate[span, :].astype(jnp.float32)).astype(jnp.bfloat16)
            result = arrivals(i) + dot(mixed, col_wo[...])
            if rows == 0:
                result_ref[span, :] = result
            else:
                both = [result_ref[span, :], result]
                both = [part.reshape(lines, ROWS, channels) for part in both]
                out_ref[pl.ds(pl.multiple_of(i * lines, lines), lines)] = (
                    jnp.concatenate(both, axis=1).astype(jnp.bfloat16)
                )

    for send in sends:
        part, block, target = send
        gather_copy(part, at(block), at(target), number[send]).wait_send()

    @pl.loop(1, peers)
    def _(step):
        for rows in range(2):
            for piece in range(pieces):
                turn_copy(rows, (me + step) % peers, me, piece).wait_send()


def both_attentions(pair_state, pair_weight, state, tokens, residue_mask, sequence_mask, table, weights):
    sequences, residues, channels = state.shape
    rows_each = pair_state.shape[0]
    peers = residues // rows_each
    everyone = peers * sequences
    pairs = sequences // 2
    block = (2, peers, pairs, 2 * ROWS, channels)
    first, steps = gather_plan()
    count = len(first) + sum(len(step[2]) for step in steps)
    whole = pl.BlockSpec(memory_space=pltpu.VMEM)
    bf16, f32 = jnp.bfloat16, jnp.float32
    return pl.pallas_call(
        kernel,
        out_shape=jax.ShapeDtypeStruct((everyone, rows_each, channels), bf16),
        in_specs=[whole] * 2 + [pl.BlockSpec(memory_space=pl.ANY)] + [whole] * 14,
        out_specs=whole,
        scratch_shapes=[
            pltpu.VMEM((sequences, residues, channels), bf16),
            pltpu.VMEM((2, peers, HEADS * ROWS, residues), bf16),
            pltpu.VMEM((sequences, 2, peers * ROWS, channels), f32),
            pltpu.VMEM((sequences, 2, peers * ROWS, channels), bf16),
            pltpu.VMEM((sequences, residues, channels), bf16),
            pltpu.VMEM((sequences, residues, channels), bf16),
            pltpu.VMEM((sequences, 2, peers * ROWS, channels), bf16),
            pltpu.VMEM((HEADS, peers * ROWS, residues), f32),
            pltpu.VMEM(block, bf16),
            pltpu.VMEM(block, bf16),
            pltpu.VMEM((2, everyone * ROWS, 128), f32),
            pltpu.VMEM((2, everyone * ROWS, 128), f32),
            pltpu.VMEM((2, everyone * ROWS, 128), f32),
            pltpu.VMEM((everyone * ROWS, channels), bf16),
            pltpu.VMEM((GROUP, everyone, 128), bf16),
            pltpu.VMEM((everyone * ROWS, channels), f32),
            pltpu.SemaphoreType.DMA,
            pltpu.SemaphoreType.DMA((count,)),
            pltpu.SemaphoreType.DMA((2, 2, peers)),
            pltpu.SemaphoreType.DMA((2, peers, pairs // PIECE)),
            pltpu.SemaphoreType.DMA((2, peers, pairs // PIECE)),
        ],
        compiler_params=pltpu.CompilerParams(
            vmem_limit_bytes=VMEM_LIMIT, collective_id=0, has_side_effects=True
        ),
        name="both_attentions",
    )(pair_state, pair_weight, state, tokens, residue_mask, sequence_mask, table, *weights)


def body(
    alignment_state,
    token_index_grid,
    sequence_mask,
    residue_mask,
    pair_state,
    token_embedding_table,
    pair_bias_weight,
    row_query_weight,
    row_key_weight,
    row_value_weight,
    row_gate_weight,
    row_output_weight,
    column_query_weight,
    column_key_weight,
    column_value_weight,
    column_gate_weight,
    column_output_weight,
):
    return both_attentions(
        pair_state, pair_bias_weight.T, alignment_state, token_index_grid, residue_mask[None, :],
        sequence_mask[None, :], token_embedding_table,
        (row_query_weight, row_key_weight, row_value_weight, row_gate_weight, row_output_weight,
         column_query_weight, column_key_weight, column_value_weight, column_gate_weight,
         column_output_weight),
    )


def solution(mesh):
    split = P(("dp", "dap"), None, None)
    in_specs = (
        split, P(("dp", "dap"), None), P("dp"), P("dp"), split,
    ) + (P(),) * 12
    return jax.shard_map(
        body, mesh=mesh, in_specs=in_specs, out_specs=P("dp", "dap", None), check_vma=False
    )
```

time: 357 us -> 99.9 us (0.28)
  matrix products: 165 us -> 0 us
  waiting for transfers between devices: 100 us -> 0 us
  Pallas kernels: 0 us -> 96.7 us
  other arithmetic: 39.8 us -> 0 us
  local copies, waits for them, and re-layouts: 31.2 us -> 3.05 us
  between operations: 13.7 us -> 0.01 us
  starting transfers between devices: 4.66 us -> 0 us
    pallas_call x0 -> x1, Pallas kernels: none -> 96.7 us  [both_attentions(): pl.pallas_call(kernel, out_shape=jax.ShapeDtypeStruct((everyone, rows_eac...]
    dot_general x18 -> x0, matrix products: 87 us -> none  [the longest x8 44.8 us: attend_block(): jnp.einsum('bhqk,bkhd->bqhd', attn_probs, valued, preferred_element_type=...]
    sub x8 -> x0, matrix products: 78.5 us -> none  [attend_block(): attn_probs = jax.nn.softmax(scores, axis=-1).astype(jnp.bfloat16)]
    all_gather x1 -> x0, waiting for transfers between devices: 73.2 us -> none  [body(): full_bias = lax.all_gather(bias_local, 'dap', axis=1, tiled=True)]
    all_to_all x1 -> x0, waiting for transfers between devices: 27 us -> none  [body(): lax.all_to_all(blocks, 'dap', split_axis=1, concat_axis=0, tiled=True)]
    convert_element_type x5 -> x0, other arithmetic: 26.8 us -> none  [the longest x4 26.3 us: attend_block(): scores = scores + bias_rows[None].astype(jnp.float32)]
    reduce_sum x5 -> x0, other arithmetic: 12.9 us -> none  [the longest x3 8.16 us: normalize(): variance = jnp.mean(centered * centered, axis=-1, keepdims=True)]
    reshape x3 -> x0, local copies, waits for them, and re-layouts: 12.4 us -> none  [the longest x2 10.8 us: grouped_attend(): return results.reshape((count,) + results.shape[2:])]
  transfers between devices with their start and end apart: 2 -> 0, of which waited for: 2 -> 0; matrix products, arithmetic and copies ran while one was open for 3% -> 0% of each run, Pallas kernels for 0% -> 0%
where the time goes in v3:
time: 99.9 us; the launch traced here: 99.8 us
  Pallas kernels  96.7 us (97%)
  local copies, waits for them, and re-layouts  3.05 us (3%)
    pallas_call x1, Pallas kernels, both_attentions(): pl.pallas_call(kernel, out_shape=jax.ShapeDtypeStruct((everyone, rows_eac...  96.7 us
    unnamed x1, local copies, waits for them, and re-layouts  3.05 us

profile of v3, /device:TPU:0, one launch (start us, length us, event | category | flops | bytes accessed | tf_op | source)
XLA Modules:
  0.0 99.8 jit_solution(3137273828257562640)
XLA Ops:
  0.0 96.7 %both_attentions.1 = bf16[256,16,256]{2,1,0:T(8,128)(2,1)} custom-call(bf16[16,512,128]{2,1,0:T(8,128)(2,1)} %pair_ref.1, bf16[8,128]{1,0:T(8,128)(2,1)} %bitcast.3, bf16[8,512,256]{2,1,0:T(8,128)(2,1)} %state_ref.1, s32[8,512]{1,0:T(8,128)} %token_ref.1, s32[1,512]{1,0:T(1,128)} %bitcast.4, s32[1,256]{1,0:T(1,128)} %bitcast.5, bf16[23,256]{1,0:T(8,128)(2,1)} %table_ref.1, ...), custom_call_target="tpu_custom_call" | custom-call | tf_op jit(solution)/shard_map/both_attentions/pallas_call | solution.py:369
  96.7 3.0 %copy.19 = bf16[256,16,256]{2,1,0:T(8,128)(2,1)} copy(bf16[256,16,256]{2,1,0:T(8,128)(2,1)} %both_attentions.1) | data formatting | bytes 4194304

commit v4 on v3

--- a/solution.py
+++ b/solution.py
@@ -18,7 +18,7 @@
 PIECE = 2
 COLUMNS = 2
 LATER = 2.5
-PROJECT_STEPS = (6, 8, 8, 8, 8, 8, 8, 8)
+PROJECT_STEPS = (0, 6, 10, 10, 10, 10, 10, 12)
 ATTEND_STEPS = (20, 20, 22, 0)
 XS, ZS, YS = 4, 2, 4
 MESH = pl.DeviceIdType.MESH
@@ -77,7 +77,7 @@
     for rows in range(2):
         for half in range(2):
             part = (rows, half)
-            for target in ((0, 1, 0), (1, 0, 0), (-1, 0, 0), (0, 0, 1), (0, 0, -1)):
+            for target in ((1, 0, 0), (-1, 0, 0), (2, 0, 0), (0, 1, 0), (0, 0, 1), (0, 0, -1), (0, 0, 2)):
                 first.append((part, (0, 0, 0), place(half, *target)))
             for u in (0, 1, -1, 2):
                 for z in range(2):
@@ -85,18 +85,10 @@
                         if (u, z, v) == (0, 0, 0):
                             continue
                         to = []
+                        if v == 0 and z == 0:
+                            to.append((0, 1, 0))
                         if v == 0:
-                            if u == 0:
-                                to += [(1, 0, 0), (-1, 0, 0)]
-                            if (u, z) == (-1, 0):
-                                to.append((1, 0, 0))
-                            if (u, z) == (1, 1):
-                                to.append((-1, 0, 0))
-                            to += [(0, 0, 1), (0, 0, -1)]
-                        if (z, v) == (0, -1):
-                            to.append((0, 0, 1))
-                        if (z, v) == (1, 1):
-                            to.append((0, 0, -1))
+                            to += [(0, 0, 1), (0, 0, -1), (0, 0, 2)]
                         hops = abs(u) + abs(v) + 1.5 * z
                         order = hops + LATER * rows + (0 if to else 0.75)
                         steps.append((order, part, place(half, u, z, v), [place(half, *t) for t in to]))

time: 99.9 us -> 92.1 us (0.922)
  Pallas kernels: 96.7 us -> 88.9 us
    pallas_call x1, Pallas kernels: 96.7 us -> 88.9 us  [both_attentions(): pl.pallas_call(kernel, out_shape=jax.ShapeDtypeStruct((everyone, rows_eac...]
where the time goes in v4:
time: 92.1 us; the launch traced here: 92 us
  Pallas kernels  88.9 us (97%)
  local copies, waits for them, and re-layouts  3.05 us (3%)
    pallas_call x1, Pallas kernels, both_attentions(): pl.pallas_call(kernel, out_shape=jax.ShapeDtypeStruct((everyone, rows_eac...  88.9 us
    unnamed x1, local copies, waits for them, and re-layouts  3.05 us

profile of v4, /device:TPU:0, one launch (start us, length us, event | category | flops | bytes accessed | tf_op | source)
XLA Modules:
  0.0 92.0 jit_solution(18432482255667949817)
XLA Ops:
  0.0 88.9 %both_attentions.1 = bf16[256,16,256]{2,1,0:T(8,128)(2,1)} custom-call(bf16[16,512,128]{2,1,0:T(8,128)(2,1)} %pair_ref.1, bf16[8,128]{1,0:T(8,128)(2,1)} %bitcast.3, bf16[8,512,256]{2,1,0:T(8,128)(2,1)} %state_ref.1, s32[8,512]{1,0:T(8,128)} %token_ref.1, s32[1,512]{1,0:T(1,128)} %bitcast.4, s32[1,256]{1,0:T(1,128)} %bitcast.5, bf16[23,256]{1,0:T(8,128)(2,1)} %table_ref.1, ...), custom_call_target="tpu_custom_call" | custom-call | tf_op jit(solution)/shard_map/both_attentions/pallas_call | solution.py:361
  88.9 3.0 %copy.19 = bf16[256,16,256]{2,1,0:T(8,128)(2,1)} copy(bf16[256,16,256]{2,1,0:T(8,128)(2,1)} %both_attentions.1) | data formatting | bytes 4194304

commit v5 on v4

--- a/solution.py
+++ b/solution.py
@@ -16,10 +16,8 @@
 MASKED = -1e9
 ROWS = 8
 PIECE = 2
-COLUMNS = 2
-LATER = 2.5
-PROJECT_STEPS = (0, 6, 10, 10, 10, 10, 10, 12)
-ATTEND_STEPS = (20, 20, 22, 0)
+COLUMNS = 4
+RELAY_AFTER = (((0, 1), 1), ((1, 0), 4), ((1, 1), 6))
 XS, ZS, YS = 4, 2, 4
 MESH = pl.DeviceIdType.MESH
 VMEM_LIMIT = 60 * 1024 * 1024
@@ -90,27 +88,22 @@
                         if v == 0:
                             to += [(0, 0, 1), (0, 0, -1), (0, 0, 2)]
                         hops = abs(u) + abs(v) + 1.5 * z
-                        order = hops + LATER * rows + (0 if to else 0.75)
+                        order = hops
                         steps.append((order, part, place(half, u, z, v), [place(half, *t) for t in to]))
     steps.sort(key=lambda step: step[:3])
     return first, [step[1:] for step in steps]
 
 
-def fill_slots(steps):
-    slots, place = {}, 0
-    room = [("project", s, n) for s, n in enumerate(PROJECT_STEPS)]
-    room += [("attend", s, n) for s, n in enumerate(ATTEND_STEPS)]
-    for stage, s, count in room:
-        slots[stage, s] = steps[place:place + count]
-        place += count
-    rest = steps[place:]
-    early = []
-    for (stage, s), taken in slots.items():
-        if stage == "attend":
-            early += [step for step in taken if step[0][0] == 0]
-            slots[stage, s] = [step for step in taken if step[0][0] == 1]
-    early += [step for step in rest if step[0][0] == 0]
-    return slots, early, [step for step in rest if step[0][0] == 1]
+def split_steps(steps):
+    relays = {(rows, level): [] for rows in range(2) for level in range(2)}
+    waits = ([], [])
+    for step in steps:
+        (rows, _), block, to = step
+        if to:
+            relays[rows, block[1]].append(step)
+        else:
+            waits[rows].append(step)
+    return relays, waits
 
 
 def kernel(
@@ -118,7 +111,7 @@
     row_wq, row_wk, row_wv, row_wg, row_wo, col_wq, col_wk, col_wv, col_wg, col_wo,
     out_ref,
     local_ref, bias_ref, embedded_ref, query_ref, key_ref, value_ref, gate_ref, wide_ref,
-    updated_ref, arrived_ref, col_query, col_key, col_value, col_gate, live_ref, result_ref,
+    updated_ref, arrived_ref, column_ref, live_ref,
     local_sem, gather_send, gather_recv, turn_send, turn_recv,
 ):
     sequences, residues, channels = local_ref.shape
@@ -184,7 +177,8 @@
             if send[0][0] == rows:
                 start(send)
 
-    slots, early, rest = fill_slots(steps)
+    relays, waits = split_steps(steps)
+    run(relays[0, 0])
     load.wait()
 
     def by_half(values):
@@ -205,9 +199,8 @@
         key_ref[s] = dot(normed, row_wk[...]).astype(jnp.bfloat16)
         value_ref[s] = dot(normed, row_wv[...]).astype(jnp.bfloat16)
         gate_ref[s] = by_half(sigmoid(dot(normed, row_wg[...]))).astype(jnp.bfloat16)
-        for k in range(sequences):
-            if slots["project", k]:
-                pl.when(s == k)(functools.partial(run, slots["project", k]))
+        for which, k in RELAY_AFTER:
+            pl.when(s == k)(functools.partial(run, relays[which]))
 
     real = residue_mask_ref[...] > 0
     pairs = sequences // 2
@@ -221,12 +214,12 @@
             device_id={"dap": target}, device_id_type=MESH,
         )
 
-    run(early)
+    run(waits[0])
 
     @pl.loop(0, 2)
     def _(rows):
-        if rest:
-            pl.when(rows == 1)(functools.partial(run, rest))
+        pl.when(rows == 1)(functools.partial(run, waits[1]))
+
         for head in range(0, HEADS, 2):
             both = bias_ref[rows, :, ROWS * head:ROWS * (head + 2), :].astype(jnp.float32) * LOG2E
             for i in range(2):
@@ -250,9 +243,6 @@
                 results.append(updated.reshape(peers, ROWS, channels))
             updated_ref[rows, :, p] = jnp.concatenate(results, axis=1).astype(jnp.bfloat16)
             arrived_ref[rows, me, p] = updated_ref[rows, me, p]
-            for k in range(pairs):
-                if slots["attend", k]:
-                    pl.when((rows == 0) & (p == k))(functools.partial(run, slots["attend", k]))
 
             @pl.when(p % PIECE == PIECE - 1)
             def _():
@@ -269,14 +259,10 @@
         live_ref[inner] = real.astype(jnp.bfloat16) * head_lanes(inner)
     real = jnp.concatenate([real, real], axis=1)
 
+    def span_of(i):
+        return pl.ds(pl.multiple_of(i * tokens, tokens), tokens)
+
     for rows in range(2):
-        def arrivals(i):
-            part = arrived_ref[rows, pl.ds(i * sources, sources)]
-            return part.astype(jnp.float32).reshape(tokens, channels)
-
-        def span_of(i):
-            return pl.ds(pl.multiple_of(i * tokens, tokens), tokens)
-
         @pl.loop(0, peers // sources)
         def _(i):
             for j in range(sources):
@@ -286,55 +272,53 @@
                 def _():
                     for piece in range(pieces):
                         turn_copy(rows, source, source, piece).wait_recv()
-            span = span_of(i)
-            normed = normalize(arrivals(i)).astype(jnp.bfloat16)
-            queries = dot(normed, col_wq[...]) * (HEAD_DIM ** -0.5 * LOG2E)
-            keyed = dot(normed, col_wk[...])
-            valued = dot(normed, col_wv[...])
+            part = arrived_ref[rows, pl.ds(i * sources, sources)]
+            part = part.astype(jnp.float32).reshape(tokens, channels)
             for half in range(2):
-                lanes = slice(128 * half, 128 * (half + 1))
-                col_query[half, span, :] = queries[:, lanes]
-                col_key[half, span, :] = keyed[:, lanes]
-                col_value[half, span, :] = valued[:, lanes]
-            col_gate[span, :] = sigmoid(dot(normed, col_wg[...])).astype(jnp.bfloat16)
+                column_ref[rows, half, span_of(i), :] = part[:, 128 * half:128 * (half + 1)]
 
         @pl.loop(0, ROWS // COLUMNS)
         def _(i):
             spans = [pl.ds(i * COLUMNS + j, everyone, stride=ROWS) for j in range(COLUMNS)]
-
-            def line(ref, span):
-                return jnp.concatenate([ref[half, span, :] for half in range(2)], axis=1)
-
-            loaded = [[line(ref, span) for ref in (col_query, col_key, col_value)] for span in spans]
+            updated = jnp.concatenate([
+                jnp.concatenate([column_ref[rows, half, span, :] for half in range(2)], axis=1)
+                for span in spans
+            ], axis=0)
+            normed = normalize(updated).astype(jnp.bfloat16)
+            queries = dot(normed, col_wq[...]) * (HEAD_DIM ** -0.5 * LOG2E)
+            queries = queries.astype(jnp.bfloat16)
+            all_keyed = dot(normed, col_wk[...])
+            all_valued = dot(normed, col_wv[...])
+            gate = sigmoid(dot(normed, col_wg[...]))
             results = []
-            for queries, keyed, valued in loaded:
+            for j in range(COLUMNS):
+                mine = slice(everyone * j, everyone * (j + 1))
+                keyed = all_keyed[mine]
                 keyed = jnp.where(real > 0.0, keyed, keyed[0:1, :]).astype(jnp.bfloat16)
-                valued = (valued * real).astype(jnp.bfloat16)
+                valued = (all_valued[mine] * real).astype(jnp.bfloat16)
                 results.append(attend(
-                    queries.astype(jnp.bfloat16),
+                    queries[mine],
                     lambda g: keyed[:, 128 * g:128 * (g + 1)],
                     lambda g: valued[:, 128 * g:128 * (g + 1)],
                     lambda inner: live_ref[inner],
                     None,
                 ))
-            for span, attended in zip(spans, results):
+            mixed = (jnp.concatenate(results, axis=0) * gate).astype(jnp.bfloat16)
+            result = updated + dot(mixed, col_wo[...])
+            for j, span in enumerate(spans):
+                mine = slice(everyone * j, everyone * (j + 1))
                 for half in range(2):
-                    col_query[half, span, :] = attended[:, 128 * half:128 * (half + 1)]
-
-        @pl.loop(0, peers // sources)
-        def _(i):
-            span = span_of(i)
-            attended = jnp.concatenate([col_query[half, span, :] for half in range(2)], axis=1)
-            mixed = (attended * col_gate[span, :].astype(jnp.float32)).astype(jnp.bfloat16)
-            result = arrivals(i) + dot(mixed, col_wo[...])
-            if rows == 0:
-                result_ref[span, :] = result
-            else:
-                both = [result_ref[span, :], result]
-                both = [part.reshape(lines, ROWS, channels) for part in both]
-                out_ref[pl.ds(pl.multiple_of(i * lines, lines), lines)] = (
-                    jnp.concatenate(both, axis=1).astype(jnp.bfloat16)
-                )
+                    column_ref[rows, half, span, :] = result[mine, 128 * half:128 * (half + 1)]
+
+    @pl.loop(0, peers // sources)
+    def _(i):
+        both = []
+        for rows in range(2):
+            halves = [column_ref[rows, half, span_of(i), :] for half in range(2)]
+            both.append(jnp.concatenate(halves, axis=1).reshape(lines, ROWS, channels))
+        out_ref[pl.ds(pl.multiple_of(i * lines, lines), lines)] = (
+            jnp.concatenate(both, axis=1).astype(jnp.bfloat16)
+        )
 
     for send in sends:
         part, block, target = send
@@ -374,12 +358,8 @@
             pltpu.VMEM((HEADS, peers * ROWS, residues), f32),
             pltpu.VMEM(block, bf16),
             pltpu.VMEM(block, bf16),
-            pltpu.VMEM((2, everyone * ROWS, 128), f32),
-            pltpu.VMEM((2, everyone * ROWS, 128), f32),
-            pltpu.VMEM((2, everyone * ROWS, 128), f32),
-            pltpu.VMEM((everyone * ROWS, channels), bf16),
+            pltpu.VMEM((2, 2, everyone * ROWS, 128), f32),
             pltpu.VMEM((GROUP, everyone, 128), bf16),
-            pltpu.VMEM((everyone * ROWS, channels), f32),
             pltpu.SemaphoreType.DMA,
             pltpu.SemaphoreType.DMA((count,)),
             pltpu.SemaphoreType.DMA((2, 2, peers)),

time: 92.1 us -> 88 us (0.955)
  Pallas kernels: 88.9 us -> 84.8 us
    pallas_call x1, Pallas kernels: 88.9 us -> 84.8 us  [both_attentions(): pl.pallas_call(kernel, out_shape=jax.ShapeDtypeStruct((everyone, rows_eac...]
where the time goes in v5:
time: 88 us; the launch traced here: 87.8 us
  Pallas kernels  84.8 us (96%)
  local copies, waits for them, and re-layouts  3.05 us (3%)
    pallas_call x1, Pallas kernels, both_attentions(): pl.pallas_call(kernel, out_shape=jax.ShapeDtypeStruct((everyone, rows_eac...  84.8 us
    unnamed x1, local copies, waits for them, and re-layouts  3.05 us

profile of v5, /device:TPU:0, one launch (start us, length us, event | category | flops | bytes accessed | tf_op | source)
XLA Modules:
  0.0 87.8 jit_solution(8495761878783633131)
XLA Ops:
  0.0 84.8 %both_attentions.1 = bf16[256,16,256]{2,1,0:T(8,128)(2,1)} custom-call(bf16[16,512,128]{2,1,0:T(8,128)(2,1)} %pair_ref.1, bf16[8,128]{1,0:T(8,128)(2,1)} %bitcast.3, bf16[8,512,256]{2,1,0:T(8,128)(2,1)} %state_ref.1, s32[8,512]{1,0:T(8,128)} %token_ref.1, s32[1,512]{1,0:T(1,128)} %bitcast.4, s32[1,256]{1,0:T(1,128)} %bitcast.5, bf16[23,256]{1,0:T(8,128)(2,1)} %table_ref.1, ...), custom_call_target="tpu_custom_call" | custom-call | tf_op jit(solution)/shard_map/both_attentions/pallas_call | solution.py:345
  84.8 3.0 %copy.19 = bf16[256,16,256]{2,1,0:T(8,128)(2,1)} copy(bf16[256,16,256]{2,1,0:T(8,128)(2,1)} %both_attentions.1) | data formatting | bytes 4194304

commit v6 on v5

--- a/solution.py
+++ b/solution.py
@@ -16,6 +16,7 @@
 MASKED = -1e9
 ROWS = 8
 PIECE = 2
+WEIGHTS = 10
 COLUMNS = 4
 RELAY_AFTER = (((0, 1), 1), ((1, 0), 4), ((1, 1), 6))
 XS, ZS, YS = 4, 2, 4
@@ -107,13 +108,16 @@
 
 
 def kernel(
-    pair_ref, pair_weight_ref, state_ref, token_ref, residue_mask_ref, sequence_mask_ref, table_ref,
-    row_wq, row_wk, row_wv, row_wg, row_wo, col_wq, col_wk, col_wv, col_wg, col_wo,
-    out_ref,
-    local_ref, bias_ref, embedded_ref, query_ref, key_ref, value_ref, gate_ref, wide_ref,
-    updated_ref, arrived_ref, column_ref, live_ref,
-    local_sem, gather_send, gather_recv, turn_send, turn_recv,
+    pair_hbm, pair_weight_ref, state_ref, token_ref, residue_mask_ref, sequence_mask_ref, table_ref,
+    *refs,
 ):
+    weights_hbm, refs = refs[:WEIGHTS], refs[WEIGHTS:]
+    (
+        out_ref,
+        pair_ref, weights_ref, local_ref, bias_ref, embedded_ref, query_ref, key_ref, value_ref, gate_ref, wide_ref,
+        updated_ref, arrived_ref, column_ref, live_ref,
+        local_sem, gather_send, gather_recv, turn_send, turn_recv,
+    ) = refs
     sequences, residues, channels = local_ref.shape
     rows_each, _, pair_channels = pair_ref.shape
     peers = residues // rows_each
@@ -124,8 +128,20 @@
         dx, dz, dy = offset
         return (((x + dx) % XS) * ZS + (z + dz) % ZS) * YS + (y + dy) % YS
 
-    load = pltpu.make_async_copy(state_ref, local_ref, local_sem)
-    load.start()
+    half_rows = [pl.ds(ROWS * rows, ROWS) for rows in range(2)]
+    load_pair = [
+        pltpu.make_async_copy(pair_hbm.at[half_rows[i]], pair_ref.at[half_rows[i]], local_sem.at[i])
+        for i in range(2)
+    ]
+    load = pltpu.make_async_copy(state_ref, local_ref, local_sem.at[2])
+    load_weights = [
+        pltpu.make_async_copy(weights_hbm[i], weights_ref.at[i], local_sem.at[3 + i])
+        for i in range(WEIGHTS)
+    ]
+    for copy in load_pair + [load] + load_weights:
+        copy.start()
+    row_wq, row_wk, row_wv, row_wg, row_wo = [weights_ref.at[i] for i in range(5)]
+    col_wq, col_wk, col_wv, col_wg, col_wo = [weights_ref.at[i] for i in range(5, WEIGHTS)]
     barrier = pltpu.get_barrier_semaphore()
     for step in range(1, peers):
         pl.semaphore_signal(
@@ -161,6 +177,7 @@
     spread = spread.reshape(HEADS * ROWS, pair_channels)
     row_of = lax.broadcasted_iota(jnp.int32, spread.shape, 0) % ROWS
     for rows in range(2):
+        load_pair[rows].wait()
         total = None
         for row in range(ROWS):
             block = pair_ref[rows * ROWS + row]
@@ -180,6 +197,8 @@
     relays, waits = split_steps(steps)
     run(relays[0, 0])
     load.wait()
+    for copy in load_weights:
+        copy.wait()
 
     def by_half(values):
         return jnp.swapaxes(values.reshape(peers, 2, ROWS, channels), 0, 1).reshape(
@@ -226,11 +245,11 @@
                 part = both[:, ROWS * i:ROWS * (i + 1), :].reshape(peers * ROWS, residues)
                 wide_ref[head + i] = jnp.where(real, part, MASKED)
 
-        @pl.loop(0, pairs)
-        def _(p):
+        @pl.loop(0, pieces)
+        def _(piece):
             results = []
-            for i in range(2):
-                s = 2 * p + i
+            for i in range(2 * PIECE):
+                s = 2 * PIECE * piece + i
                 attended = attend(
                     query_ref[s, rows],
                     lambda g: key_ref[s, :, 128 * g:128 * (g + 1)],
@@ -241,13 +260,13 @@
                 mixed = (attended * gate_ref[s, rows].astype(jnp.float32)).astype(jnp.bfloat16)
                 updated = embedded_ref[s, rows] + dot(mixed, row_wo[...])
                 results.append(updated.reshape(peers, ROWS, channels))
-            updated_ref[rows, :, p] = jnp.concatenate(results, axis=1).astype(jnp.bfloat16)
-            arrived_ref[rows, me, p] = updated_ref[rows, me, p]
-
-            @pl.when(p % PIECE == PIECE - 1)
-            def _():
-                for step in range(1, peers):
-                    turn_copy(rows, (me + step) % peers, me, p // PIECE).start()
+            for i in range(PIECE):
+                p = piece * PIECE + i
+                both = jnp.concatenate(results[2 * i:2 * i + 2], axis=1)
+                updated_ref[rows, :, p] = both.astype(jnp.bfloat16)
+                arrived_ref[rows, me, p] = updated_ref[rows, me, p]
+            for step in range(1, peers):
+                turn_copy(rows, (me + step) % peers, me, piece).start()
 
     tokens = 512
     lines = tokens // ROWS
@@ -341,13 +360,16 @@
     first, steps = gather_plan()
     count = len(first) + sum(len(step[2]) for step in steps)
     whole = pl.BlockSpec(memory_space=pltpu.VMEM)
+    hbm = pl.BlockSpec(memory_space=pl.ANY)
     bf16, f32 = jnp.bfloat16, jnp.float32
     return pl.pallas_call(
         kernel,
         out_shape=jax.ShapeDtypeStruct((everyone, rows_each, channels), bf16),
-        in_specs=[whole] * 2 + [pl.BlockSpec(memory_space=pl.ANY)] + [whole] * 14,
+        in_specs=[hbm, whole, hbm] + [whole] * 4 + [hbm] * WEIGHTS,
         out_specs=whole,
         scratch_shapes=[
+            pltpu.VMEM(pair_state.shape, bf16),
+            pltpu.VMEM((WEIGHTS, channels, channels), bf16),
             pltpu.VMEM((sequences, residues, channels), bf16),
             pltpu.VMEM((2, peers, HEADS * ROWS, residues), bf16),
             pltpu.VMEM((sequences, 2, peers * ROWS, channels), f32),
@@ -360,7 +382,7 @@
             pltpu.VMEM(block, bf16),
             pltpu.VMEM((2, 2, everyone * ROWS, 128), f32),
             pltpu.VMEM((GROUP, everyone, 128), bf16),
-            pltpu.SemaphoreType.DMA,
+            pltpu.SemaphoreType.DMA((3 + WEIGHTS,)),
             pltpu.SemaphoreType.DMA((count,)),
             pltpu.SemaphoreType.DMA((2, 2, peers)),
             pltpu.SemaphoreType.DMA((2, peers, pairs // PIECE)),

time: 88 us -> 86 us (0.977)
  Pallas kernels: 84.8 us -> 82.7 us
    pallas_call x1, Pallas kernels: 84.8 us -> 82.7 us  [both_attentions(): pl.pallas_call(kernel, out_shape=jax.ShapeDtypeStruct((everyone, rows_eac...]
where the time goes in v6:
time: 86 us; the launch traced here: 85.8 us
  Pallas kernels  82.7 us (96%)
  local copies, waits for them, and re-layouts  3.05 us (4%)
    pallas_call x1, Pallas kernels, both_attentions(): pl.pallas_call(kernel, out_shape=jax.ShapeDtypeStruct((everyone, rows_eac...  82.7 us
    unnamed x1, local copies, waits for them, and re-layouts  3.05 us

profile of v6, /device:TPU:0, one launch (start us, length us, event | category | flops | bytes accessed | tf_op | source)
XLA Modules:
  0.0 85.8 jit_solution(13334858773819724735)
XLA Ops:
  0.0 82.7 %both_attentions.1 = bf16[256,16,256]{2,1,0:T(8,128)(2,1)} custom-call(bf16[16,512,128]{2,1,0:T(8,128)(2,1)} %pair_hbm.1, bf16[8,128]{1,0:T(8,128)(2,1)} %bitcast.3, bf16[8,512,256]{2,1,0:T(8,128)(2,1)} %state_ref.1, s32[8,512]{1,0:T(8,128)} %token_ref.1, s32[1,512]{1,0:T(1,128)} %bitcast.4, s32[1,256]{1,0:T(1,128)} %bitcast.5, bf16[23,256]{1,0:T(8,128)(2,1)} %table_ref.1, ...), custom_call_target="tpu_custom_call" | custom-call | tf_op jit(solution)/shard_map/both_attentions/pallas_call | solution.py:365
  82.8 3.0 %copy.19 = bf16[256,16,256]{2,1,0:T(8,128)(2,1)} copy(bf16[256,16,256]{2,1,0:T(8,128)(2,1)} %both_attentions.1) | data formatting | bytes 4194304

commit v7 on v6

--- a/solution.py
+++ b/solution.py
@@ -17,8 +17,8 @@
 ROWS = 8
 PIECE = 2
 WEIGHTS = 10
-COLUMNS = 4
-RELAY_AFTER = (((0, 1), 1), ((1, 0), 4), ((1, 1), 6))
+COLUMNS = 8
+RELAY_AFTER = (((0, 1), 0), ((1, 0), 1), ((1, 1), 2))
 XS, ZS, YS = 4, 2, 4
 MESH = pl.DeviceIdType.MESH
 VMEM_LIMIT = 60 * 1024 * 1024
@@ -205,21 +205,22 @@
             2, peers * ROWS, channels
         )
 
-    @pl.loop(0, sequences)
-    def _(s):
-        tokens = token_ref[pl.ds(s, 1), :]
-        kinds = lax.broadcasted_iota(jnp.int32, (TOKEN_KINDS, residues), 0)
-        indicator = (kinds == tokens).astype(jnp.float32).astype(jnp.bfloat16)
-        embedded = local_ref[s].astype(jnp.float32) + dot(indicator, table_ref[...], TN)
-        embedded_ref[s] = by_half(embedded)
-        normed = normalize(embedded).astype(jnp.bfloat16)
-        queries = dot(normed, row_wq[...]) * (HEAD_DIM ** -0.5 * LOG2E)
-        query_ref[s] = by_half(queries).astype(jnp.bfloat16)
-        key_ref[s] = dot(normed, row_wk[...]).astype(jnp.bfloat16)
-        value_ref[s] = dot(normed, row_wv[...]).astype(jnp.bfloat16)
-        gate_ref[s] = by_half(sigmoid(dot(normed, row_wg[...]))).astype(jnp.bfloat16)
+    @pl.loop(0, sequences // 2)
+    def _(pair):
+        for s in (2 * pair, 2 * pair + 1):
+            tokens = token_ref[pl.ds(s, 1), :]
+            kinds = lax.broadcasted_iota(jnp.int32, (TOKEN_KINDS, residues), 0)
+            indicator = (kinds == tokens).astype(jnp.float32).astype(jnp.bfloat16)
+            embedded = local_ref[s].astype(jnp.float32) + dot(indicator, table_ref[...], TN)
+            embedded_ref[s] = by_half(embedded)
+            normed = normalize(embedded).astype(jnp.bfloat16)
+            queries = dot(normed, row_wq[...]) * (HEAD_DIM ** -0.5 * LOG2E)
+            query_ref[s] = by_half(queries).astype(jnp.bfloat16)
+            key_ref[s] = dot(normed, row_wk[...]).astype(jnp.bfloat16)
+            value_ref[s] = dot(normed, row_wv[...]).astype(jnp.bfloat16)
+            gate_ref[s] = by_half(sigmoid(dot(normed, row_wg[...]))).astype(jnp.bfloat16)
         for which, k in RELAY_AFTER:
-            pl.when(s == k)(functools.partial(run, relays[which]))
+            pl.when(pair == k)(functools.partial(run, relays[which]))
 
     real = residue_mask_ref[...] > 0
     pairs = sequences // 2

time: 86 us -> 85.8 us (level)
  no operation moved by 1% of the time
where the time goes in v7:
time: 85.8 us; the launch traced here: 85.6 us
  Pallas kernels  82.6 us (96%)
  local copies, waits for them, and re-layouts  3.05 us (4%)
    pallas_call x1, Pallas kernels, both_attentions(): pl.pallas_call(kernel, out_shape=jax.ShapeDtypeStruct((everyone, rows_eac...  82.6 us
    unnamed x1, local copies, waits for them, and re-layouts  3.05 us

profile of v7, /device:TPU:0, one launch (start us, length us, event | category | flops | bytes accessed | tf_op | source)
XLA Modules:
  0.0 85.6 jit_solution(17247816933284424175)
XLA Ops:
  0.0 82.6 %both_attentions.1 = bf16[256,16,256]{2,1,0:T(8,128)(2,1)} custom-call(bf16[16,512,128]{2,1,0:T(8,128)(2,1)} %pair_hbm.1, bf16[8,128]{1,0:T(8,128)(2,1)} %bitcast.3, bf16[8,512,256]{2,1,0:T(8,128)(2,1)} %state_ref.1, s32[8,512]{1,0:T(8,128)} %token_ref.1, s32[1,512]{1,0:T(1,128)} %bitcast.4, s32[1,256]{1,0:T(1,128)} %bitcast.5, bf16[23,256]{1,0:T(8,128)(2,1)} %table_ref.1, ...), custom_call_target="tpu_custom_call" | custom-call | tf_op jit(solution)/shard_map/both_attentions/pallas_call | solution.py:366
  82.6 3.0 %copy.19 = bf16[256,16,256]{2,1,0:T(8,128)(2,1)} copy(bf16[256,16,256]{2,1,0:T(8,128)(2,1)} %both_attentions.1) | data formatting | bytes 4194304
